TPU v7x, 256 devices: a whole 4x4x8 slice. The times are simulated.
256 devices in a mesh: dp: 64 (over z, y, core), fsdp: 4 (over x).
Axes of the slice: x: 4, y: 4, z: 8, core: 2. Of those that a mesh axis runs over, the one named last changes fastest.
Arguments:
- projections: bfloat16 [512, 192, 4608], P(('dp', 'fsdp')), may hold values from -10 to 10
- residual_in: bfloat16 [512, 192, 1536], P(('dp', 'fsdp')), may hold values from -3 to 3
- velocity_target: bfloat16 [512, 128, 64], P(('dp', 'fsdp')), may hold values from -6 to 6
- out_weight: bfloat16 [1536, 1536], P(None, 'fsdp'), may hold values from -0.15625 to 0.15625
- final_weight: bfloat16 [1536, 64], replicated, may hold values from -0.15625 to 0.15625
- modulation: bfloat16 [32, 4608], replicated, may hold values from -3 to 3
- bucket_sizes: int32 [512], replicated, may hold values from 32 to 128, as said below
- liked: int32 [512], replicated, may hold values 0 or 1
- timesteps: int32 [512], replicated, may hold values from 0 to 31
- reference_error: float32 [512], replicated, may hold values from 0.7 to 5.7
- move_list: int32 [4, 32, 2], P('fsdp'), may hold values from 0 to 63, as said below
Outputs:
- out_weight_grad: float32 [1536, 1536], P('dp', 'fsdp')
- projection_grad: bfloat16 [768, 192, 4608], P(('dp', 'fsdp'))
- slot_loss: float32 [768], P(('dp', 'fsdp'))
Inputs may be any that keep to these rules, and one draw needn't show every extreme that they name: `bucket_sizes`: a multiple of a quarter of 128. `move_list`: in each fsdp column every dp index stands in exactly one pair, as source or as destination; a pair's source has summed bucket sizes no smaller than its destination's.
All inputs are finite; a program needn't handle non-finite values.
Results may differ from a plain program's by a relative error of at most 0.012.
Values may be sent and summed in bfloat16 or wider, within the bound.
A program may use at most 128 MiB of HBM per device.

v0:
```python
import math

import jax
import jax.numpy as jnp
from jax import lax
from jax.sharding import PartitionSpec as P

HEADS = 12
HD = 128
IMG_DEV = 2


reward_scale = 2.0
loss_scale = 4096.0
norm_epsilon = 1e-06


def longest_slot(bucket_sizes, device, per_device):
    local_sizes = lax.dynamic_slice_in_dim(bucket_sizes, device * per_device, per_device)
    ranking = local_sizes * per_device + (per_device - 1 - jnp.arange(per_device, dtype=jnp.int32))
    return jnp.argmax(ranking)


def route_image(flat_image, sources, destinations):
    senders = lax.axis_size("dp")
    spread = lax.all_to_all(
        flat_image.reshape(senders, -1), "dp", split_axis=0, concat_axis=0, tiled=True
    )
    target_of = jnp.arange(senders, dtype=jnp.int32)[:, None] == destinations[None, :]
    sender_rank = jnp.sum(jnp.where(target_of, sources[None, :], 0), axis=1)
    wanted = jnp.any(target_of, axis=1)
    picked = jnp.where(
        wanted[:, None], jnp.take(spread, sender_rank, axis=0), jnp.zeros((), spread.dtype)
    )
    arrived = lax.all_to_all(picked, "dp", split_axis=0, concat_axis=0, tiled=True)
    return arrived.reshape(-1)


def image_pass(
    slot_proj,
    slot_resid,
    slot_target,
    image_sizes,
    liked_slot,
    steps_slot,
    ref_slot,
    modulation,
    full_weight,
    final_weight,
):
    slot_count = slot_proj.shape[0]
    sequence = slot_proj.shape[1]
    image_tokens = slot_target.shape[1]
    text_tokens = sequence - image_tokens
    model_width = full_weight.shape[1]
    senders = lax.axis_size("dp")
    shards = lax.axis_size("fsdp")
    split_heads = slot_proj.reshape(slot_count, sequence, 3, HEADS, HD)
    queries = split_heads[:, text_tokens:, 0]
    key_rows = split_heads[:, :, 1]
    values = split_heads[:, :, 2]
    score_root = math.sqrt(HD)
    scores = (
        jnp.einsum("nqhd,nkhd->nhqk", queries, key_rows, preferred_element_type=jnp.float32)
        / score_root
    )
    live_keys = jnp.arange(sequence)[None, :] < text_tokens + image_sizes[:, None]
    scores = jnp.where(live_keys[:, None, None, :], scores, -1e30)
    highest = jnp.max(scores, axis=-1, keepdims=True)
    raised = jnp.exp(scores - highest)
    attention = raised / jnp.sum(raised, axis=-1, keepdims=True)
    attention_low = attention.astype(jnp.bfloat16)
    mixed_heads = jnp.einsum(
        "nhqk,nkhd->nqhd", attention_low, values, preferred_element_type=jnp.float32
    )
    mixed_heads = mixed_heads.reshape(slot_count, image_tokens, HEADS * HD).astype(jnp.bfloat16)
    branch = jnp.einsum("ntr,rc->ntc", mixed_heads, full_weight, preferred_element_type=jnp.float32)
    one_hot = (
        steps_slot[:, None] == jnp.arange(modulation.shape[0], dtype=jnp.int32)[None, :]
    ).astype(jnp.bfloat16)
    chosen = jnp.dot(one_hot, modulation, preferred_element_type=jnp.float32)[:, None, :]
    gate_values = chosen[:, :, :model_width]
    shift_values = chosen[:, :, model_width : 2 * model_width]
    scale_values = chosen[:, :, 2 * model_width :]
    residual_rows = slot_resid[:, text_tokens:].astype(jnp.float32) + gate_values * branch
    centered = residual_rows - jnp.mean(residual_rows, axis=-1, keepdims=True)
    inverse = lax.rsqrt(jnp.mean(centered * centered, axis=-1, keepdims=True) + norm_epsilon)
    unit_rows = centered * inverse
    normed = (unit_rows * (1.0 + scale_values) + shift_values).astype(jnp.bfloat16)
    predicted = jnp.einsum("ntc,cp->ntp", normed, final_weight, preferred_element_type=jnp.float32)
    valid_rows = (jnp.arange(image_tokens)[None, :] < image_sizes[:, None])[:, :, None]
    differ = jnp.where(valid_rows, predicted - slot_target.astype(jnp.float32), 0.0)
    divisor = final_weight.shape[1] * jnp.maximum(image_sizes, 1)
    errors = jnp.sum(differ * differ, axis=(1, 2)) / divisor
    present = image_sizes > 0
    rewards = jnp.where(present, reward_scale * (ref_slot - errors), 0.0)
    images = IMG_DEV * senders * shards
    anchor = lax.psum(jnp.sum(rewards), ("dp", "fsdp")) / images
    sign_values = (2 * liked_slot - 1).astype(jnp.float32)
    sigmoid_values = jax.nn.sigmoid(sign_values * (rewards - anchor))
    losses = jnp.where(present, 1.0 - sigmoid_values, 0.0)
    slopes = jnp.where(
        present,
        loss_scale * reward_scale * sign_values * sigmoid_values * (1.0 - sigmoid_values),
        0.0,
    )
    factor = slopes * 2.0 / divisor
    d_predicted = (factor[:, None, None] * differ).astype(jnp.bfloat16)
    d_normed = jnp.einsum(
        "ntp,cp->ntc", d_predicted, final_weight, preferred_element_type=jnp.float32
    )
    scaled = d_normed * (1.0 + scale_values)
    d_residual = inverse * (
        scaled
        - jnp.mean(scaled, axis=-1, keepdims=True)
        - unit_rows * jnp.mean(scaled * unit_rows, axis=-1, keepdims=True)
    )
    d_branch = (gate_values * d_residual).astype(jnp.bfloat16)
    weight_term = jnp.einsum(
        "ntpr,ntfc->pfrc",
        mixed_heads.reshape(slot_count, image_tokens, senders, -1),
        d_branch.reshape(slot_count, image_tokens, shards, -1),
        preferred_element_type=jnp.float32,
    )
    weight_term = weight_term.reshape(-1, weight_term.shape[3])
    weight_grad = lax.psum_scatter(weight_term, ("dp", "fsdp"), scatter_dimension=0, tiled=True)
    d_mixed = jnp.einsum(
        "ntc,rc->ntr", d_branch, full_weight, preferred_element_type=jnp.float32
    ).astype(jnp.bfloat16)
    d_heads = d_mixed.reshape(slot_count, image_tokens, HEADS, HD)
    d_attention = jnp.einsum("nqhd,nkhd->nhqk", d_heads, values, preferred_element_type=jnp.float32)
    row_totals = jnp.sum(attention * d_attention, axis=-1, keepdims=True)
    d_scores = (attention * (d_attention - row_totals) / score_root).astype(jnp.bfloat16)
    d_queries = jnp.einsum(
        "nhqk,nkhd->nqhd", d_scores, key_rows, preferred_element_type=jnp.float32
    )
    d_keys = jnp.einsum("nhqk,nqhd->nkhd", d_scores, queries, preferred_element_type=jnp.float32)
    d_values = jnp.einsum(
        "nhqk,nqhd->nkhd", attention_low, d_heads, preferred_element_type=jnp.float32
    )
    d_queries = jnp.concatenate(
        [jnp.zeros((slot_count, text_tokens, HEADS, HD), jnp.float32), d_queries], axis=1
    )
    slot_grads = (
        jnp.stack([d_queries, d_keys, d_values], axis=2)
        .reshape(slot_count, sequence, 3 * HEADS * HD)
        .astype(jnp.bfloat16)
    )
    return (slot_grads, losses, weight_grad)


def local(
    projections,
    residual_in,
    velocity_target,
    out_weight,
    final_weight,
    modulation,
    bucket_sizes,
    liked,
    timesteps,
    reference_error,
    move_list,
):
    shards = lax.axis_size("fsdp")
    own_rank = lax.axis_index("dp")
    own_shard = lax.axis_index("fsdp")
    per_device = projections.shape[0]
    device_id = own_rank * shards + own_shard
    sources = move_list[0, :, 0]
    destinations = move_list[0, :, 1]
    full_weight = lax.all_gather(out_weight, "fsdp", axis=1, tiled=True)
    is_source = jnp.any(sources == own_rank)
    is_target = jnp.any(destinations == own_rank)
    from_rank = jnp.sum(jnp.where(destinations == own_rank, sources, 0))
    out_slot = longest_slot(bucket_sizes, device_id, per_device)
    from_device = from_rank * shards + own_shard
    in_index = from_device * per_device + longest_slot(bucket_sizes, from_device, per_device)
    own_index = device_id * per_device + jnp.arange(per_device, dtype=jnp.int32)
    leaving = (jnp.arange(per_device, dtype=jnp.int32) == out_slot) & is_source
    flat_image = jnp.concatenate(
        [
            projections[out_slot].reshape(-1),
            residual_in[out_slot].reshape(-1),
            velocity_target[out_slot].reshape(-1),
        ]
    )
    flat_image = jnp.where(is_source, flat_image, jnp.zeros((), jnp.bfloat16))
    arrived = route_image(flat_image, sources, destinations)
    first_end = projections[0].size
    second_end = first_end + residual_in[0].size
    slot_proj = jnp.concatenate(
        [projections, arrived[:first_end].reshape((1,) + projections.shape[1:])], axis=0
    )
    slot_resid = jnp.concatenate(
        [residual_in, arrived[first_end:second_end].reshape((1,) + residual_in.shape[1:])], axis=0
    )
    slot_target = jnp.concatenate(
        [velocity_target, arrived[second_end:].reshape((1,) + velocity_target.shape[1:])], axis=0
    )
    slot_index = jnp.concatenate([own_index, in_index[None]])
    present = jnp.concatenate([jnp.logical_not(leaving), is_target[None]])
    image_sizes = jnp.where(present, jnp.take(bucket_sizes, slot_index), 0)
    projection_grad, slot_loss, weight_grad = image_pass(
        slot_proj,
        slot_resid,
        slot_target,
        image_sizes,
        jnp.take(liked, slot_index),
        jnp.take(timesteps, slot_index),
        jnp.take(reference_error, slot_index),
        modulation,
        full_weight,
        final_weight,
    )
    return (weight_grad, projection_grad, slot_loss)


def solution(mesh):
    in_specs = (
        P(("dp", "fsdp"), None, None),
        P(("dp", "fsdp"), None, None),
        P(("dp", "fsdp"), None, None),
        P(None, "fsdp"),
        P(),
        P(),
        P(),
        P(),
        P(),
        P(),
        P("fsdp", None, None),
    )
    out_specs = (P("dp", "fsdp"), P(("dp", "fsdp"), None, None), P(("dp", "fsdp")))
    return jax.shard_map(local, mesh=mesh, in_specs=in_specs, out_specs=out_specs, check_vma=False)
```

profile of v0, /device:TPU:4, one launch (start us, length us, event | category | flops | bytes accessed | tf_op | source)
XLA Modules:
  0.0 780.8 jit_solution(11928284828273072515)
XLA Ops:
  19.7 10.9 %maximum_select_fusion = bf16[1187840]{0:T(1024)(128)(2,1)S(1)} fusion(bf16[8192]{0:T(1024)(128)(2,1)S(1)} %reshape_squeeze.11, bf16[294912]{0:T(1024)(128)(2,1)S(1)} %reshape_squeeze.10, bf16[884736]{0:T(1024)(128)(2,1)} %reshape_squeeze.9, pred[]{:T(512)} %get-tuple-element.11), kind=kLoop, calls=%fused_computation.25 | loop fusion | flops 8314880 | bytes 4751361 | tf_op jit(solution)/shard_map/jit(_where)/select_n | solution.py:188
  30.6 3.9 select_n.161
  35.1 15.1 %reduce.33 = bf16[64,18560]{1,0:T(8,128)(2,1)S(1)} reduce(bf16[64,1,18560]{2,1,0:T(2,128)(2,1)} %select_n.161, bf16[]{:T(256)} %broadcast.425), dimensions={1}, to_apply=%select_n.161.reduce_sub_computation | reduce | bytes 4751362 | tf_op jit(solution)/shard_map/jit(_where)/select_n | solution.py:188
  53.5 12.4 %all-to-all-start = ((bf16[64,2,9280]{2,1,0:T(2,128)(2,1)}), bf16[64,2,9280]{2,1,0:T(2,128)(2,1)S(1)}, u32[]{:S(2)}, u32[]{:S(2)}) async-start(bf16[64,2,9280]{2,1,0:T(2,128)(2,1)} %reshape.330), calls=%async_computation | async-start | bytes 4784128 | tf_op jit(solution)/shard_map/all_to_all | solution.py:26
  66.9 56.7 %all-to-all-done = bf16[64,2,9280]{2,1,0:T(2,128)(2,1)S(1)} async-done(((bf16[64,2,9280]{2,1,0:T(2,128)(2,1)}), bf16[64,2,9280]{2,1,0:T(2,128)(2,1)S(1)}, u32[]{:S(2)}, u32[]{:S(2)}) %all-to-all-start) | async-done | bytes 2375712 | tf_op jit(solution)/shard_map/all_to_all | solution.py:26
  123.6 7.4 reshape.331
  142.3 4.9 reshape.332
  147.2 5.3 all-to-all-start.1
  154.0 7.3 concatenate.56
  167.8 5.1 copy_dynamic-update-slice_fusion
  172.9 37.4 %all-to-all-done.1 = bf16[64,2,9280]{2,1,0:T(2,128)(2,1)S(1)} async-done(((bf16[64,2,9280]{2,1,0:T(2,128)(2,1)}), bf16[64,2,9280]{2,1,0:T(2,128)(2,1)S(1)}, u32[]{:S(2)}, u32[]{:S(2)}) %all-to-all-start.1) | async-done | bytes 2375712 | tf_op jit(solution)/shard_map/all_to_all | solution.py:35
  210.3 7.4 reshape.333
  217.7 14.5 %reduce.29 = bf16[64,18560]{1,0:T(8,128)(2,1)S(1)} reduce(bf16[64,1,18560]{2,1,0:T(2,128)(2,1)} %reshape.333, bf16[]{:T(256)} %constant.116), dimensions={1}, to_apply=%all_to_all.12.reduce_sub_computation | reduce | bytes 4751362 | tf_op jit(solution)/shard_map/all_to_all | solution.py:35
  232.2 5.0 reshape.269
  259.0 5.1 fusion.71
  266.5 73.4 %psum.7 = f32[]{:T(128)} all-reduce(f32[]{:T(128)} %get-tuple-element.14), channel_id=1, replica_groups=mesh['dp'=64,'fsdp'=4] {'dp','fsdp'}, use_global_device_ids=true, to_apply=%region_13.15 | all-reduce | flops 1 | bytes 8 | tf_op jit(solution)/shard_map/psum | solution.py:98
  347.2 3.9 convolution_bitcast_fusion.1
  351.1 9.1 %copy.67 = f32[64,4,24,384]{3,2,1,0:T(8,128)} copy(f32[64,4,24,384]{3,0,2,1:T(8,128)S(1)} %convolution_bitcast_fusion.1) | data formatting | bytes 18874368 | tf_op jit(solution)/shard_map/ntpr,ntfc->pfrc/transpose | solution.py:119
  361.5 5.4 fusion.13
  372.7 8.5 %fusion.40 = bf16[3,128,12,128]{3,1,2,0:T(8,128)(2,1)} fusion(f32[3,12,128,192]{2,3,1,0:T(8,128)} %fusion.33, bf16[3,192,3,12,128]{4,1,3,0,2:T(8,128)(2,1)} %copy_dynamic-update-slice_fusion.1, f32[3,12,128,192]{2,3,1,0:T(8,128)} %copy-done.12, f32[3,12,128]{2,1,0:T(8,128)S(1)} %get-tuple-element.24), kind=kOutput, calls=%fused_computation.53 | convolution fusion | flops 233280192 | bytes 17154048 | tf_op jit(solution)/shard_map/nhqk,nkhd->nqhd/dot_general | solution.py:134
  382.7 8.1 %convert_bitcast_fusion.1 = bf16[3,192,1,12,128]{4,1,3,0,2:T(8,128)(2,1)} fusion(f32[3,12,128,192]{2,3,1,0:T(8,128)} %fusion.33, bf16[3,192,3,12,128]{4,1,3,0,2:T(8,128)(2,1)} %copy_dynamic-update-slice_fusion.1, f32[3,12,128,192]{2,3,1,0:T(8,128)} %copy-done.12, f32[3,12,128]{2,1,0:T(8,128)S(1)} %get-tuple-element.24), kind=kOutput, calls=%fused_computation.40 | convolution fusion | flops 233575104 | bytes 17154048 | tf_op jit(solution)/shard_map/nhqk,nqhd->nkhd/dot_general | solution.py:137
  394.6 6.5 copy.71
  401.0 10.3 %convert_element_type.64 = bf16[3,192,4608]{2,1,0:T(8,128)(2,1)} reshape(bf16[3,192,3,12,128]{4,3,2,1,0:T(8,128)(2,1)} %copy.71) | data formatting | bytes 10616832 | tf_op jit(solution)/shard_map/convert_element_type | solution.py:147
  411.3 362.5 %reduce-scatter.4.cloned.1.call-done = f32[24,384]{1,0:T(8,128)} async-done(((f32[6144,384]{1,0:T(8,128)}), f32[24,384]{1,0:T(8,128)}) %reduce-scatter.4.cloned.1.call-update) | async-done | bytes 36880
  (99 shorter events, 76.3 us)
Async XLA Ops:
  7.2 160.3 %copy-start = (bf16[32,4608]{1,0:T(8,128)(2,1)S(1)}, bf16[32,4608]{1,0:T(8,128)(2,1)}, u32[]{:S(2)}) copy-start(bf16[32,4608]{1,0:T(8,128)(2,1)} %param.18) | copy-start | bytes 884740
  53.5 13.2 %copy-start.10 = (s32[1,32,2]{1,2,0:T(2,128)S(1)}, s32[1,32,2]{1,2,0:T(2,128)}, u32[]{:S(2)}) copy-start(s32[1,32,2]{1,2,0:T(2,128)} %param.23) | copy-start | bytes 772
  53.5 70.1 %all-to-all-start = ((bf16[64,2,9280]{2,1,0:T(2,128)(2,1)}), bf16[64,2,9280]{2,1,0:T(2,128)(2,1)S(1)}, u32[]{:S(2)}, u32[]{:S(2)}) async-start(bf16[64,2,9280]{2,1,0:T(2,128)(2,1)} %reshape.330), calls=%async_computation | async-start | bytes 4784128 | tf_op jit(solution)/shard_map/all_to_all | solution.py:26
  65.9 193.1 %all-gather.2.cloned.1.call-start = ((), (), s32[]{:S(2)}) async-start(), calls=%async_computation.3 | async-start | bytes 5898240 | tf_op jit(solution)/shard_map/all_gather | solution.py:172
  147.2 63.0 %all-to-all-start.1 = ((bf16[64,2,9280]{2,1,0:T(2,128)(2,1)}), bf16[64,2,9280]{2,1,0:T(2,128)(2,1)S(1)}, u32[]{:S(2)}, u32[]{:S(2)}) async-start(bf16[64,2,9280]{2,1,0:T(2,128)(2,1)} %reshape.332), calls=%async_computation.1 | async-start | bytes 4784128 | tf_op jit(solution)/shard_map/all_to_all | solution.py:35
  152.6 621.2 %reduce-scatter.4.cloned.1.call-start = ((), (), s32[]{:S(2)}) async-start(), calls=%async_computation.4 | async-start | bytes 9474048
  153.9 7.3 copy-start.2
  154.0 9.5 %copy-start.3 = (s32[512]{0:T(512)S(1)}, s32[512]{0:T(512)}, u32[]{:S(2)}) copy-start(s32[512]{0:T(512)} %param.20) | copy-start | bytes 6148
  154.0 10.2 %copy-start.4 = (s32[512]{0:T(512)S(1)}, s32[512]{0:T(512)}, u32[]{:S(2)}) copy-start(s32[512]{0:T(512)} %param.21) | copy-start | bytes 6148
  154.0 10.8 %copy-start.5 = (f32[512]{0:T(512)S(1)}, f32[512]{0:T(512)}, u32[]{:S(2)}) copy-start(f32[512]{0:T(512)} %param.22) | copy-start | bytes 6148
  240.1 3.7 slice-start
  245.2 2.4 slice-start.1
  253.8 1.7 copy-start.12
  255.5 3.5 copy-start.7
  264.1 0.9 copy-start.9
  264.1 0.9 copy-start.11
  360.2 1.3 copy-start.6
  390.9 3.0 copy-start.8
  401.0 372.8 %copy-start.1 = (bf16[32,4608]{1,0:T(8,128)(2,1)S(1)}, bf16[32,4608]{1,0:T(8,128)(2,1)}, u32[]{:S(2)}) copy-start(bf16[32,4608]{1,0:T(8,128)(2,1)} %param.18) | copy-start | bytes 884740
Sparse Core Ops, SparseCore 0:
  68.6 55.5 all-gather.1
  360.3 413.4 reduce-scatter.3
where the time goes:
time: 791 us; the launch traced here: 781 us
  waiting for transfers between devices  457 us (58%)
  local copies, waits for them, and re-layouts  109 us (14%)
  blocking collectives  73.4 us (9%)
  other arithmetic  58.7 us (7%)
  matrix products  46 us (6%)
  between operations  18.4 us (2%)
  starting transfers between devices  17.8 us (2%)
    unnamed x3, waiting for transfers between devices  363 us
    psum x1, blocking collectives, image_pass(): anchor = lax.psum(jnp.sum(rewards), ('dp', 'fsdp')) / images  73.4 us
    all_to_all x1, waiting for transfers between devices, route_image(): lax.all_to_all(flat_image.reshape(senders, -1), 'dp', split_axis=0, conca...  56.7 us
    all_to_all x1, waiting for transfers between devices, route_image(): lax.all_to_all(picked, 'dp', split_axis=0, concat_axis=0, tiled=True)  37.4 us
    unnamed x33, local copies, waits for them, and re-layouts  34.4 us
    select_n x2, other arithmetic, local(): flat_image = jnp.where(is_source, flat_image, jnp.zeros((), jnp.bfloat16))  26 us
  transfers between devices with their start and end apart: 4, of which 3 were waited for; matrix products, arithmetic and copies ran while one was open for 18% of the time, Pallas kernels for 0%

commit v1 on v0

v1 whole, which is shorter than its diff:
```python
import functools
import math

import jax
import jax.numpy as jnp
from jax import lax
from jax.experimental import pallas as pl
from jax.experimental.pallas import tpu as pltpu
from jax.sharding import PartitionSpec as P

HEADS = 12
HD = 128
D = 1536
PATCH = 64
TXT = 64
LMAX = 128
SEQ = 192
IMAGES = 512
NZ, NY, NC, NX = 8, 4, 2, 4
COLS = D // NX
HALF = D // NC
PART = 24
GROUP = 4

REWARD_SCALE = 2.0
LOSS_SCALE = 4096.0
EPSILON = 1e-06
MESH = pl.DeviceIdType.MESH
F32 = jnp.float32
BF16 = jnp.bfloat16
VMEM_LIMIT = 56 * 1024 * 1024

ANY = pl.BlockSpec(memory_space=pl.ANY)
VMEM = pl.BlockSpec(memory_space=pltpu.VMEM)
SMEM = pl.BlockSpec(memory_space=pltpu.SMEM)


def place():
    rank = lax.axis_index("dp")
    return rank // (NY * NC), (rank // NC) % NY, rank % NC, lax.axis_index("fsdp")


def device(z, y, c, x):
    return ((z * NY + y) * NC + c, x)


def greet(partners):
    barrier = pltpu.get_barrier_semaphore()
    for partner in partners:
        pl.semaphore_signal(barrier, inc=1, device_id=partner, device_id_type=MESH)
    pl.semaphore_wait(barrier, len(partners))


def remote(src, dst, send, recv, target):
    return pltpu.make_async_remote_copy(
        src_ref=src, dst_ref=dst, send_sem=send, recv_sem=recv, device_id=target, device_id_type=MESH
    )


def dot(a, b, left, right):
    return lax.dot_general(a, b, (((left,), (right,)), ((), ())), preferred_element_type=F32)


def rows_of(start, size, step):
    return pl.ds(pl.multiple_of(start, step), size)


def longest(sizes, dev):
    return jnp.where(sizes[2 * dev] >= sizes[2 * dev + 1], 0, 1)


def image_kernel(
    proj_hbm, resid_hbm, weight_hbm, target, final, modulation, sizes, steps,
    grad_a, grad_b, mixed, d_branch, errors,
    proj, resid, weight, attention, branch, d_mixed,
    load_sem, w_send, w_recv, e_send, e_recv,
):
    z, y, c, x = place()
    dev = lax.axis_index("dp") * NX + x
    sibling = device(z, y, 1 - c, x)
    right, left = (x + 1) % NX, (x + NX - 1) % NX
    opposite = (x + 2) % NX
    others_x = [device(z, y, c, (x + k) % NX) for k in range(1, NX)]
    others_y = [device(z, (y + k) % NY, c, x) for k in range(1, NY)]
    others_z = [device((z + k) % NZ, y, c, x) for k in range(1, NZ)]

    load_proj = pltpu.make_async_copy(proj_hbm, proj, load_sem.at[0])
    load_proj.start()
    load_resid = pltpu.make_async_copy(resid_hbm.at[:, pl.ds(TXT, LMAX)], resid, load_sem.at[1])
    load_resid.start()
    load_weight = pltpu.make_async_copy(weight_hbm, weight.at[x], load_sem.at[2])
    load_weight.start()

    greet([sibling] + others_x + others_y + others_z)

    half = rows_of(c * HALF, HALF, 16)
    upper = rows_of(c * HALF, HALF // 2, 16)
    lower = rows_of(c * HALF + HALF // 2, HALF // 2, 16)
    mine = weight_hbm.at[half]
    to_right = remote(mine, weight.at[x, half], w_send.at[0], w_recv.at[0], device(z, y, c, right))
    to_left = remote(mine, weight.at[x, half], w_send.at[1], w_recv.at[1], device(z, y, c, left))
    to_right.start()
    to_left.start()
    load_proj.wait()

    first = longest(sizes, dev)
    root = 1.0 / math.sqrt(HD)
    key_index = lax.broadcasted_iota(jnp.int32, (LMAX, SEQ), 1)

    def head_forward(i, slot, size, h):
        cols = pl.multiple_of(h * HD, HD)
        q = proj[slot, pl.ds(TXT, LMAX), pl.ds(cols, HD)]
        k = proj[slot, :, pl.ds(D + cols, HD)]
        v = proj[slot, :, pl.ds(2 * D + cols, HD)]
        scores = dot(q, k, 1, 1) * root
        scores = jnp.where(key_index < TXT + size, scores, -1e30)
        raised = jnp.exp(scores - jnp.max(scores, axis=-1, keepdims=True))
        probs = raised * (1.0 / jnp.sum(raised, axis=-1, keepdims=True))
        attention[i, h] = probs
        mixed[rows_of(i * LMAX, LMAX, 16), pl.ds(cols, HD)] = dot(probs.astype(BF16), v, 1, 0).astype(BF16)

    def forward_group(n, carry):
        i = n // (HEADS // GROUP)
        slot = jnp.where(i == 0, first, 1 - first)
        size = sizes[2 * dev + slot]
        for j in range(GROUP):
            head_forward(i, slot, size, (n % (HEADS // GROUP)) * GROUP + j)
        return carry

    lax.fori_loop(0, 2 * HEADS // GROUP, forward_group, 0)

    to_right.wait_recv()
    on_right = remote(weight.at[left, upper], weight.at[left, upper], w_send.at[2], w_recv.at[2], device(z, y, c, right))
    on_right.start()
    to_left.wait_recv()
    on_left = remote(weight.at[right, lower], weight.at[right, lower], w_send.at[3], w_recv.at[3], device(z, y, c, left))
    on_left.start()
    across = []
    for n, owner in enumerate((left, right)):
        copy = remote(weight.at[owner, half], weight.at[owner, half], w_send.at[4 + n], w_recv.at[4 + n], sibling)
        copy.start()
        across.append(copy)
    load_weight.wait()
    load_resid.wait()

    def branch_part(owner):
        cols = rows_of(owner * COLS, COLS, 128)
        branch[:, cols] = dot(mixed[...], weight[owner], 1, 0)

    branch_part(x)
    across[0].wait_recv()
    branch_part(left)
    across[1].wait_recv()
    branch_part(right)
    on_right.wait_recv()
    on_left.wait_recv()
    last = remote(weight.at[opposite, half], weight.at[opposite, half], w_send.at[6], w_recv.at[6], sibling)
    last.start()
    last.wait_recv()
    branch_part(opposite)

    lane = lax.broadcasted_iota(jnp.int32, (1, 128), 1)
    row_index = lax.broadcasted_iota(jnp.int32, (PATCH, LMAX), 1)
    level = lax.broadcasted_iota(jnp.int32, (16, 32), 1)

    def image_middle(i, found):
        slot = jnp.where(i == 0, first, 1 - first)
        size = sizes[2 * dev + slot]
        chosen = dot((level == steps[2 * dev + slot]).astype(F32).astype(BF16), modulation[...], 1, 0)[0:1]
        gate = chosen[:, :D]
        shift = chosen[:, D : 2 * D]
        scale = 1.0 + chosen[:, 2 * D :]
        rows = rows_of(i * LMAX, LMAX, 16)
        residual = resid[slot].astype(F32) + gate * branch[rows]
        centered = residual - jnp.mean(residual, axis=-1, keepdims=True)
        inverse = lax.rsqrt(jnp.mean(centered * centered, axis=-1, keepdims=True) + EPSILON)
        unit = centered * inverse
        normed = (unit * scale + shift).astype(BF16)
        predicted = dot(final[...], normed, 1, 1)
        differ = jnp.where(row_index < size, predicted - target[slot].astype(F32), 0.0)
        divisor = jnp.full((1, 1), PATCH * size, jnp.int32).astype(F32)
        squares = jnp.sum(jnp.sum(differ * differ, axis=1, keepdims=True), axis=0, keepdims=True)
        d_predicted = (differ * (2.0 / divisor)).astype(BF16)
        scaled = dot(d_predicted, final[...], 0, 0) * scale
        d_residual = inverse * (
            scaled
            - jnp.mean(scaled, axis=-1, keepdims=True)
            - unit * jnp.mean(scaled * unit, axis=-1, keepdims=True)
        )
        d_branch[rows, :] = (gate * d_residual).astype(BF16)
        return found + jnp.where(lane == slot, squares / divisor, 0.0)

    errors[z, y, x, c] = lax.fori_loop(0, 2, image_middle, jnp.zeros((1, 128), F32))

    e_core = remote(errors.at[z, y, x, c], errors.at[z, y, x, c], e_send.at[0], e_recv.at[0], sibling)
    e_core.start()

    total = dot(d_branch[:, pl.ds(0, COLS)], weight[0], 1, 1)
    for owner in range(1, NX):
        total += dot(d_branch[:, pl.ds(owner * COLS, COLS)], weight[owner], 1, 1)
    d_mixed[...] = total.astype(BF16)

    e_core.wait_recv()
    e_x = [
        remote(errors.at[z, y, x], errors.at[z, y, x], e_send.at[k], e_recv.at[k], others_x[k - 1])
        for k in range(1, NX)
    ]
    for copy in e_x:
        copy.start()

    def head_backward(i, slot, h, grads):
        cols = pl.multiple_of(h * HD, HD)
        q = proj[slot, pl.ds(TXT, LMAX), pl.ds(cols, HD)]
        k = proj[slot, :, pl.ds(D + cols, HD)]
        v = proj[slot, :, pl.ds(2 * D + cols, HD)]
        d_head = d_mixed[rows_of(i * LMAX, LMAX, 16), pl.ds(cols, HD)]
        probs = attention[i, h]
        d_probs = dot(d_head, v, 1, 1)
        totals = jnp.sum(probs * d_probs, axis=-1, keepdims=True)
        d_scores = (probs * (d_probs - totals) * root).astype(BF16)
        side = h // (HEADS // 2)
        out_cols = rows_of((h % (HEADS // 2)) * HD, HD, 128)
        d_q = dot(d_scores, k, 1, 0).astype(BF16)
        d_k = dot(d_scores, q, 0, 0).astype(BF16)
        d_v = dot(probs.astype(BF16), d_head, 0, 0).astype(BF16)
        grads[side, 0:8, :, out_cols] = d_q.reshape(8, 16, HD)
        grads[side, 8:20, :, out_cols] = d_k.reshape(12, 16, HD)
        grads[side, 20:32, :, out_cols] = d_v.reshape(12, 16, HD)

    def backward(i, slot, grads):
        def group(n, carry):
            for j in range(GROUP):
                head_backward(i, slot, n * GROUP + j, grads)
            return carry

        lax.fori_loop(0, HEADS // GROUP, group, 0)

    backward(0, first, grad_a)

    for copy in e_x:
        copy.wait_recv()
    e_y = [
        remote(errors.at[z, y], errors.at[z, y], e_send.at[3 + k], e_recv.at[3 + k], others_y[k - 1])
        for k in range(1, NY)
    ]
    for copy in e_y:
        copy.start()

    backward(1, 1 - first, grad_b)

    for copy in e_y:
        copy.wait_recv()
    e_z = [
        remote(errors.at[z], errors.at[z], e_send.at[6 + k], e_recv.at[6 + k], others_z[k - 1])
        for k in range(1, NZ)
    ]
    for copy in e_z:
        copy.start()
    for copy in e_z:
        copy.wait_recv()
    for copy in [to_right, to_left, on_right, on_left, last, e_core] + across + e_x + e_y + e_z:
        copy.wait_send()


def image_pass(projections, residual_in, velocity_target, out_weight, final_weight, modulation, sizes, steps):
    grads = jax.ShapeDtypeStruct((2, 32, 16, HEADS // 2 * HD), BF16)
    return pl.pallas_call(
        image_kernel,
        name="images",
        out_shape=(
            grads,
            grads,
            jax.ShapeDtypeStruct((2 * LMAX, D), BF16),
            jax.ShapeDtypeStruct((2 * LMAX, D), BF16),
            jax.ShapeDtypeStruct((NZ, NY, NX, NC, 1, 128), F32),
        ),
        in_specs=[ANY, ANY, ANY, VMEM, VMEM, VMEM, SMEM, SMEM],
        out_specs=(VMEM,) * 5,
        scratch_shapes=[
            pltpu.VMEM((2, SEQ, 3 * D), BF16),
            pltpu.VMEM((2, LMAX, D), BF16),
            pltpu.VMEM((NX, D, COLS), BF16),
            pltpu.VMEM((2, HEADS, LMAX, SEQ), F32),
            pltpu.VMEM((2 * LMAX, D), F32),
            pltpu.VMEM((2 * LMAX, D), BF16),
            pltpu.SemaphoreType.DMA((3,)),
            pltpu.SemaphoreType.DMA((7,)),
            pltpu.SemaphoreType.DMA((7,)),
            pltpu.SemaphoreType.DMA((14,)),
            pltpu.SemaphoreType.DMA((14,)),
        ],
        compiler_params=pltpu.CompilerParams(
            collective_id=0, has_side_effects=True, vmem_limit_bytes=VMEM_LIMIT
        ),
        cost_estimate=pl.CostEstimate(flops=4_500_000_000, bytes_accessed=20_000_000, transcendentals=600_000),
    )(projections, residual_in, out_weight, velocity_target, final_weight, modulation, sizes, steps)


def anchor_of(errors, reference):
    flat = errors[...].reshape(NZ * NY * NX * NC, 128)
    total = jnp.sum(jnp.sum(flat, axis=0, keepdims=True), axis=1, keepdims=True)
    known = jnp.sum(jnp.sum(reference[...], axis=0, keepdims=True), axis=1, keepdims=True)
    return REWARD_SCALE * (known - total) / IMAGES


def loss_of(error_row, slot, known, liked, anchor):
    lane = lax.broadcasted_iota(jnp.int32, (1, 128), 1)
    error = jnp.sum(jnp.where(lane == slot, error_row, 0.0), axis=1, keepdims=True)
    sign = jnp.full((1, 1), 2 * liked - 1, jnp.int32).astype(F32)
    reward = REWARD_SCALE * (jnp.full((1, 1), known, F32) - error)
    sig = jax.nn.sigmoid(sign * (reward - anchor))
    return 1.0 - sig, LOSS_SCALE * REWARD_SCALE * sign * sig * (1.0 - sig)


def weight_kernel(
    mixed, d_branch, errors, reference, sizes, liked, known,
    out,
    scaled, term, core_send, core_recv, own, far_send, far_recv, near_send, near_recv, y_total,
    far_send_y, far_recv_y, near_send_y, near_recv_y, z_send, z_recv,
    c_sems, x_sems, y_sems, z_sems,
):
    z, y, c, x = place()
    dev = lax.axis_index("dp") * NX + x
    sibling = device(z, y, 1 - c, x)
    right_x, left_x = (x + 1) % NX, (x + NX - 1) % NX
    right_y, left_y = (y + 1) % NY, (y + NY - 1) % NY
    x_pair = (device(z, y, c, right_x), device(z, y, c, left_x))
    y_pair = (device(z, right_y, c, x), device(z, left_y, c, x))
    others_z = [device((z + k) % NZ, y, c, x) for k in range(1, NZ)]
    greet([sibling, *x_pair, *y_pair] + others_z)

    anchor = anchor_of(errors, reference)
    row = errors[z, y, x, c]
    first = longest(sizes, dev)
    for i in range(2):
        slot = first if i == 0 else 1 - first
        index = 2 * dev + slot
        _, slope = loss_of(row, slot, known[index], liked[index], anchor)
        rows = pl.ds(i * LMAX, LMAX)
        scaled[rows, :] = (d_branch[rows, :].astype(F32) * slope).astype(BF16)

    def make(owner):
        term[...] = dot(mixed[...], scaled[:, rows_of(owner * COLS, COLS, 128)], 0, 0)
        for yy in range(NY):
            for core, target in ((1 - c, core_send), (c, own)):
                parts = [
                    term[rows_of(((zz * NY + yy) * NC + core) * PART, PART, 8), :] for zz in range(NZ)
                ]
                block = jnp.concatenate(parts, axis=0)
                target[owner, pl.ds(yy * NZ * PART, NZ * PART), :] = block.astype(target.dtype)
        copy = remote(core_send.at[owner], core_recv.at[owner], c_sems.at[0, owner], c_sems.at[1, owner], sibling)
        copy.start()
        return copy

    opposite = (x + 2) % NX
    owners = (opposite, right_x, left_x, x)
    copies = [make(owner) for owner in owners]

    def chip_total(n):
        copies[n].wait_recv()
        own[owners[n]] = own[owners[n]] + core_recv[owners[n]].astype(F32)

    def ring(pair, sems, far, rights, lefts, far_out, far_in, near_out, near_in, size):
        middle = size // 2
        outer = []
        for n in range(2):
            far_out[n] = far(pl.ds(n * middle, middle)).astype(BF16)
            copy = remote(far_out.at[n], far_in.at[n], sems.at[0, n], sems.at[1, n], pair[n])
            copy.start()
            outer.append(copy)
        inner = []
        for n, near in ((0, rights), (1, lefts)):
            block = near()
            outer[n].wait_recv()
            for part in range(2):
                rows = pl.ds(part * middle, middle)
                piece = block(rows)
                if part == n:
                    piece = piece + far_in[n].astype(F32)
                near_out[n, rows, :] = piece.astype(BF16)
            copy = remote(near_out.at[n], near_in.at[n], sems.at[0, 2 + n], sems.at[1, 2 + n], pair[n])
            copy.start()
            inner.append(copy)
        return outer, inner

    chip_total(0)

    def near_x(n):
        def get():
            chip_total(n)
            return lambda rows: own[owners[n], rows, :]

        return get

    outer_x, inner_x = ring(
        x_pair, x_sems, lambda rows: own[opposite, rows, :], near_x(1), near_x(2),
        far_send, far_recv, near_send, near_recv, HALF,
    )
    chip_total(3)
    inner_x[0].wait_recv()
    inner_x[1].wait_recv()
    own[x] = own[x] + near_recv[0].astype(F32) + near_recv[1].astype(F32)

    strip = NZ * PART

    def y_rows(which, rows):
        return own[x, pl.ds(pl.multiple_of(which * strip, 16) + rows.start, rows.size), :]

    outer_y, inner_y = ring(
        y_pair, y_sems, lambda rows: y_rows((y + 2) % NY, rows),
        lambda: lambda rows: y_rows(right_y, rows), lambda: lambda rows: y_rows(left_y, rows),
        far_send_y, far_recv_y, near_send_y, near_recv_y, strip,
    )
    inner_y[0].wait_recv()
    inner_y[1].wait_recv()
    y_total[...] = (
        y_rows(y, pl.ds(0, strip)) + near_recv_y[0].astype(F32) + near_recv_y[1].astype(F32)
    )
    for zz in range(NZ):
        z_send[zz] = y_total[pl.ds(zz * PART, PART), :]
    z_copies = []
    for k in range(1, NZ):
        copy = remote(
            z_send.at[(z + k) % NZ], z_recv.at[k - 1], z_sems.at[0, k - 1], z_sems.at[1, k - 1], others_z[k - 1]
        )
        copy.start()
        z_copies.append(copy)
    total = z_send[z]
    for k, copy in enumerate(z_copies):
        copy.wait_recv()
        total = total + z_recv[k]
    out[...] = total
    for copy in copies + outer_x + inner_x + outer_y + inner_y + z_copies:
        copy.wait_send()


def weight_pass(mixed, d_branch, errors, reference, sizes, liked, known):
    strip = NZ * PART
    return pl.pallas_call(
        weight_kernel,
        name="weight",
        out_shape=jax.ShapeDtypeStruct((PART, COLS), F32),
        in_specs=[VMEM, VMEM, VMEM, VMEM, SMEM, SMEM, SMEM],
        out_specs=VMEM,
        scratch_shapes=[
            pltpu.VMEM((2 * LMAX, D), BF16),
            pltpu.VMEM((D, COLS), F32),
            pltpu.VMEM((NX, HALF, COLS), BF16),
            pltpu.VMEM((NX, HALF, COLS), BF16),
            pltpu.VMEM((NX, HALF, COLS), F32),
            pltpu.VMEM((2, HALF // 2, COLS), BF16),
            pltpu.VMEM((2, HALF // 2, COLS), BF16),
            pltpu.VMEM((2, HALF, COLS), BF16),
            pltpu.VMEM((2, HALF, COLS), BF16),
            pltpu.VMEM((strip, COLS), F32),
            pltpu.VMEM((2, strip // 2, COLS), BF16),
            pltpu.VMEM((2, strip // 2, COLS), BF16),
            pltpu.VMEM((2, strip, COLS), BF16),
            pltpu.VMEM((2, strip, COLS), BF16),
            pltpu.VMEM((NZ, PART, COLS), F32),
            pltpu.VMEM((NZ - 1, PART, COLS), F32),
            pltpu.SemaphoreType.DMA((2, NX)),
            pltpu.SemaphoreType.DMA((2, 4)),
            pltpu.SemaphoreType.DMA((2, 4)),
            pltpu.SemaphoreType.DMA((2, NZ - 1)),
        ],
        compiler_params=pltpu.CompilerParams(
            collective_id=1, has_side_effects=True, vmem_limit_bytes=VMEM_LIMIT
        ),
        cost_estimate=pl.CostEstimate(flops=1_200_000_000, bytes_accessed=60_000_000, transcendentals=10),
    )(mixed, d_branch, errors, reference, sizes, liked, known)


def place_kernel(rank_ref, moves, sizes, liked, known, grad_a, grad_b, arrived, errors, reference, out, losses):
    rank = rank_ref[0]
    x = rank_ref[1]
    dev = rank * NX + x
    slot = pl.program_id(0)

    def look(n, found):
        source, goal = moves[2 * n], moves[2 * n + 1]
        leaving, origin = found
        return jnp.where(source == rank, 1, leaving), jnp.where(goal == rank, source, origin)

    leaving, origin = lax.fori_loop(0, moves.shape[0] // 2, look, (jnp.int32(0), jnp.int32(-1)))
    anchor = anchor_of(errors, reference)
    first = longest(sizes, dev)
    is_new = slot == 2
    from_rank = jnp.where(is_new, jnp.maximum(origin, 0), rank)
    from_dev = from_rank * NX + x
    from_slot = jnp.where(is_new, longest(sizes, from_dev), slot)
    index = 2 * from_dev + from_slot
    row = errors[from_rank // (NY * NC), (from_rank // NC) % NY, x, from_rank % NC]
    loss, slope = loss_of(row, from_slot, known[index], liked[index], anchor)
    goes = jnp.logical_and(leaving == 1, slot == first)
    present = jnp.where(is_new, origin >= 0, jnp.logical_not(goes))
    losses[slot] = jnp.where(present, loss[0, 0], 0.0)

    wide = HEADS // 2 * HD

    def write(grads):
        for side in range(2):
            for base, low, count, rows in ((0, 0, 8, LMAX), (D, 8, 12, SEQ), (2 * D, 20, 12, SEQ)):
                block = grads[side, low : low + count].reshape(rows, wide).astype(F32) * slope
                out[0, SEQ - rows :, base + side * wide : base + (side + 1) * wide] = block.astype(BF16)
        out[0, :TXT, :D] = jnp.zeros((TXT, D), BF16)

    @pl.when(jnp.logical_not(present))
    def _():
        out[...] = jnp.zeros_like(out)

    @pl.when(jnp.logical_and(present, is_new))
    def _():
        write(arrived)

    @pl.when(jnp.logical_and(present, slot == first))
    def _():
        write(grad_a)

    @pl.when(jnp.logical_and(present, slot == 1 - first))
    def _():
        write(grad_b)


def place_pass(place_of, moves, sizes, liked, known, grad_a, grad_b, arrived, errors, reference):
    return pl.pallas_call(
        place_kernel,
        name="slots",
        grid=(3,),
        out_shape=(jax.ShapeDtypeStruct((3, SEQ, 3 * D), BF16), jax.ShapeDtypeStruct((3,), F32)),
        in_specs=[SMEM] * 5 + [VMEM] * 5,
        out_specs=(pl.BlockSpec((1, SEQ, 3 * D), lambda i: (i, 0, 0)), SMEM),
        compiler_params=pltpu.CompilerParams(vmem_limit_bytes=VMEM_LIMIT),
        cost_estimate=pl.CostEstimate(flops=3_000_000, bytes_accessed=10_000_000, transcendentals=10),
    )(place_of, moves, sizes, liked, known, grad_a, grad_b, arrived, errors, reference)


def local(
    projections, residual_in, velocity_target, out_weight, final_weight, modulation,
    bucket_sizes, liked, timesteps, reference_error, move_list,
):
    rank = lax.axis_index("dp")
    senders = lax.axis_size("dp")
    reference = reference_error.reshape(4, 128)
    moves = move_list.reshape(-1)
    place_of = jnp.stack([rank, lax.axis_index("fsdp")]).astype(jnp.int32)
    grad_a, grad_b, mixed, d_branch, errors = image_pass(
        projections, residual_in, jnp.swapaxes(velocity_target, 1, 2), out_weight, final_weight.T,
        modulation, bucket_sizes, timesteps,
    )
    spread = lax.all_to_all(
        grad_a.reshape(senders, 16, -1), "dp", split_axis=0, concat_axis=0, tiled=True
    )
    target_of = jnp.arange(senders, dtype=jnp.int32)[:, None] == move_list[0, :, 1][None, :]
    sender_rank = jnp.sum(jnp.where(target_of, move_list[0, :, 0][None, :], 0), axis=1)
    picked = jnp.take(spread, sender_rank, axis=0, mode="clip")
    arrived = lax.all_to_all(picked, "dp", split_axis=0, concat_axis=0, tiled=True)
    weight_grad = weight_pass(mixed, d_branch, errors, reference, bucket_sizes, liked, reference_error)
    projection_grad, slot_loss = place_pass(
        place_of, moves, bucket_sizes, liked, reference_error,
        grad_a, grad_b, arrived.reshape(grad_a.shape), errors, reference,
    )
    return (weight_grad, projection_grad, slot_loss)


def solution(mesh):
    in_specs = (
        P(("dp", "fsdp"), None, None),
        P(("dp", "fsdp"), None, None),
        P(("dp", "fsdp"), None, None),
        P(None, "fsdp"),
        P(),
        P(),
        P(),
        P(),
        P(),
        P(),
        P("fsdp", None, None),
    )
    out_specs = (P("dp", "fsdp"), P(("dp", "fsdp"), None, None), P(("dp", "fsdp")))
    return jax.shard_map(local, mesh=mesh, in_specs=in_specs, out_specs=out_specs, check_vma=False)
```

time: 791 us -> 172 us (0.22); the launches traced: 781 us -> 172 us
  waiting for transfers between devices: 457 us -> 40 us
  Pallas kernels: 0 us -> 112 us
  local copies, waits for them, and re-layouts: 109 us -> 4.27 us
  blocking collectives: 73.4 us -> 0 us
  other arithmetic: 58.7 us -> 0.77 us
  matrix products: 46 us -> 0 us
  between operations: 18.4 us -> 0.7 us
    unnamed x3 -> x0, waiting for transfers between devices: 363 us -> none
    pallas_call x0 -> x3, Pallas kernels: none -> 112 us  [the longest x1 53.1 us: weight_pass(): pl.pallas_call(weight_kernel, name='weight', out_shape=jax.ShapeDtypeStru...]
    psum x1 -> x0, blocking collectives: 73.4 us -> none  [image_pass(): anchor = lax.psum(jnp.sum(rewards), ('dp', 'fsdp')) / images]
    all_to_all x2, waiting for transfers between devices: 94.1 us -> 40 us  [the longest x1 40 us: local(): lax.all_to_all(grad_a.reshape(senders, 16, -1), 'dp', split_axis=0, conca...]
    dot_general x12 -> x0, matrix products: 46 us -> none  [the longest x1 8.5 us: image_pass(): jnp.einsum('nhqk,nkhd->nqhd', d_scores, key_rows, preferred_element_type=...]
    unnamed x33 -> x8, local copies, waits for them, and re-layouts: 34.4 us -> 1.86 us
    select_n x8 -> x0, other arithmetic: 32 us -> none  [the longest x2 26 us: local(): flat_image = jnp.where(is_source, flat_image, jnp.zeros((), jnp.bfloat16))]
    all_to_all x1 -> x0, other arithmetic: 14.5 us -> none  [route_image(): lax.all_to_all(picked, 'dp', split_axis=0, concat_axis=0, tiled=True)]
  transfers between devices with their start and end apart: 4 -> 2, of which waited for: 3 -> 1; matrix products, arithmetic and copies ran while one was open for 18% -> 1% of each run, Pallas kernels for 0% -> 31%
where the time goes in v1:
time: 172 us
  Pallas kernels  112 us (65%)
  waiting for transfers between devices  40 us (23%)
  starting transfers between devices  13.8 us (8%)
  local copies, waits for them, and re-layouts  4.27 us (2%)
    pallas_call x1, Pallas kernels, weight_pass(): pl.pallas_call(weight_kernel, name='weight', out_shape=jax.ShapeDtypeStru...  53.1 us
    pallas_call x1, Pallas kernels, image_pass(): pl.pallas_call(image_kernel, name='images', out_shape=(grads, grads, jax....  52.9 us
    all_to_all x1, waiting for transfers between devices, local(): lax.all_to_all(grad_a.reshape(senders, 16, -1), 'dp', split_axis=0, conca...  40 us
    all_to_all x1, starting transfers between devices, local(): lax.all_to_all(grad_a.reshape(senders, 16, -1), 'dp', split_axis=0, conca...  8.33 us
    pallas_call x1, Pallas kernels, place_pass(): pl.pallas_call(place_kernel, name='slots', grid=(3,), out_shape=(jax.Shap...  6.37 us
    all_to_all x1, starting transfers between devices, local(): lax.all_to_all(picked, 'dp', split_axis=0, concat_axis=0, tiled=True)  5.52 us
  transfers between devices with their start and end apart: 2, of which 1 were waited for; matrix products, arithmetic and copies ran while one was open for 1% of the time, Pallas kernels for 31%

profile of v1, /device:TPU:4, one launch (start us, length us, event | category | flops | bytes accessed | tf_op | source)
XLA Modules:
  0.0 172.0 jit_solution(16262319191020296109)
XLA Ops:
  0.6 52.9 %images.1 = (bf16[2,32,16,768]{3,2,1,0:T(8,128)(2,1)}, bf16[2,32,16,768]{3,2,1,0:T(8,128)(2,1)}, bf16[256,1536]{1,0:T(8,128)(2,1)}, bf16[256,1536]{1,0:T(8,128)(2,1)}, f32[8,4,4,2,1,128]{5,4,3,2,1,0:T(1,128)}) custom-call(bf16[2,192,4608]{2,1,0:T(8,128)(2,1)} %proj_hbm.1, bf16[2,192,1536]{2,1,0:T(8,128)(2,1)} %resid_hbm.1, bf16[1536,384]{1,0:T(8,128)(2,1)} %weight_hbm.1, ...), custom_call_target="tpu_custom_call" | custom-call | flops 4499999744 | bytes 20000000 | tf_op jit(solution)/shard_map/images/pallas_call | solution.py:267
  53.5 0.0 copy-start.2
  53.6 8.3 %all-to-all-start = ((bf16[64,16,768]{2,1,0:T(8,128)(2,1)}), bf16[64,16,768]{2,1,0:T(8,128)(2,1)S(1)}, u32[]{:S(2)}, u32[]{:S(2)}) async-start(bf16[64,16,768]{2,1,0:T(8,128)(2,1)} %bitcast.11), calls=%async_computation | async-start | bytes 3145728 | tf_op jit(solution)/shard_map/all_to_all | solution.py:551
  61.9 0.0 copy-done.2
  61.9 0.1 select_reduce_fusion
  62.0 40.0 %all-to-all-done = bf16[64,16,768]{2,1,0:T(8,128)(2,1)S(1)} async-done(((bf16[64,16,768]{2,1,0:T(8,128)(2,1)}), bf16[64,16,768]{2,1,0:T(8,128)(2,1)S(1)}, u32[]{:S(2)}, u32[]{:S(2)}) %all-to-all-start) | async-done | bytes 1572896 | tf_op jit(solution)/shard_map/all_to_all | solution.py:551
  102.0 1.8 %gather_fusion = bf16[64,16,768]{2,1,0:T(8,128)(2,1)} fusion(bf16[64,16,768]{2,1,0:T(8,128)(2,1)S(1)} %all-to-all-done, s32[1024]{0:T(1024)S(1)} %pad_clamp_fusion), kind=kCustom, calls=%fused_computation | custom fusion | bytes 3145984 | tf_op jit(solution)/shard_map/jit(_take)/gather | solution.py:556
  103.8 5.5 %all-to-all-start.1 = ((bf16[64,16,768]{2,1,0:T(8,128)(2,1)}), bf16[64,16,768]{2,1,0:T(8,128)(2,1)S(1)}, u32[]{:S(2)}, u32[]{:S(2)}) async-start(bf16[64,16,768]{2,1,0:T(8,128)(2,1)} %gather_fusion), calls=%async_computation.1 | async-start | bytes 3145728 | tf_op jit(solution)/shard_map/all_to_all | solution.py:557
  109.3 0.1 copy.16
  109.4 0.6 reshape.21.moves
  110.0 53.1 %weight.1 = f32[24,384]{1,0:T(8,128)} custom-call(bf16[256,1536]{1,0:T(8,128)(2,1)} %get-tuple-element.10.mixed, bf16[256,1536]{1,0:T(8,128)(2,1)} %get-tuple-element.11.d_branch, f32[8,4,4,2,1,128]{5,4,3,2,1,0:T(1,128)} %get-tuple-element.12.errors, f32[4,128]{1,0:T(4,128)} %bitcast.13, s32[512]{0:T(512)} %sizes.5, s32[512]{0:T(512)} %liked.3, f32[512]{0:T(512)} %known.3), custom_call_target="tpu_custom_call" | custom-call | flops 1200000000 | bytes 60000000 | tf_op jit(solution)/shard_map/weight/pallas_call | solution.py:439
  163.2 0.7 pad_add_fusion.rank_ref
  163.9 0.0 all-to-all-done.1
  163.9 0.0 copy-start
  163.9 1.1 copy-done
  165.0 0.0 copy-start.1
  165.0 6.4 %slots.1 = (bf16[3,192,4608]{2,1,0:T(8,128)(2,1)}, f32[3]{0:T(128)}) custom-call(s32[2]{0:T(128)} %pad_add_fusion.rank_ref, s32[64]{0:T(128)} %reshape.21.moves, s32[512]{0:T(512)} %sizes.5, s32[512]{0:T(512)} %liked.3, f32[512]{0:T(512)} %known.3, bf16[2,32,16,768]{3,2,1,0:T(8,128)(2,1)} %get-tuple-element.13.grad_a, ...), custom_call_target="tpu_custom_call" | custom-call | flops 3000000 | bytes 10000000 | tf_op jit(solution)/shard_map/slots/pallas_call | solution.py:526
  171.4 0.0 copy-done.1
  171.4 0.6 copy.18
  (2 shorter events, 0.0 us)
Async XLA Ops:
  53.5 8.4 %copy-start.2 = (s32[1,32,2]{1,2,0:T(2,128)S(1)}, s32[1,32,2]{1,2,0:T(2,128)}, u32[]{:S(2)}) copy-start(s32[1,32,2]{1,2,0:T(2,128)} %param.21) | copy-start | bytes 772
  53.6 48.5 %all-to-all-start = ((bf16[64,16,768]{2,1,0:T(8,128)(2,1)}), bf16[64,16,768]{2,1,0:T(8,128)(2,1)S(1)}, u32[]{:S(2)}, u32[]{:S(2)}) async-start(bf16[64,16,768]{2,1,0:T(8,128)(2,1)} %bitcast.11), calls=%async_computation | async-start | bytes 3145728 | tf_op jit(solution)/shard_map/all_to_all | solution.py:551
  103.8 60.1 %all-to-all-start.1 = ((bf16[64,16,768]{2,1,0:T(8,128)(2,1)}), bf16[64,16,768]{2,1,0:T(8,128)(2,1)S(1)}, u32[]{:S(2)}, u32[]{:S(2)}) async-start(bf16[64,16,768]{2,1,0:T(8,128)(2,1)} %gather_fusion), calls=%async_computation.1 | async-start | bytes 3145728 | tf_op jit(solution)/shard_map/all_to_all | solution.py:557
  163.9 1.2 copy-start
  165.0 6.4 %copy-start.1 = (f32[24,384]{1,0:T(8,128)S(1)}, f32[24,384]{1,0:T(8,128)}, u32[]{:S(2)}) copy-start(f32[24,384]{1,0:T(8,128)} %weight.1) | copy-start | bytes 110596

commit v2 on v1

--- a/solution.py
+++ b/solution.py
@@ -21,6 +21,11 @@
 HALF = D // NC
 PART = 24
 GROUP = 4
+DP = NZ * NY * NC
+EARLY = 8
+LATE = HEADS - EARLY
+TILE = 16
+STRIDE = 27
 
 REWARD_SCALE = 2.0
 LOSS_SCALE = 4096.0
@@ -30,6 +35,8 @@
 BF16 = jnp.bfloat16
 VMEM_LIMIT = 56 * 1024 * 1024
 
+PARTS = ((0, 0, 8, LMAX), (D, 8, 12, SEQ), (2 * D, 20, 12, SEQ))
+
 ANY = pl.BlockSpec(memory_space=pl.ANY)
 VMEM = pl.BlockSpec(memory_space=pltpu.VMEM)
 SMEM = pl.BlockSpec(memory_space=pltpu.SMEM)
@@ -69,20 +76,66 @@
     return jnp.where(sizes[2 * dev] >= sizes[2 * dev + 1], 0, 1)
 
 
-def image_kernel(
-    proj_hbm, resid_hbm, weight_hbm, target, final, modulation, sizes, steps,
-    grad_a, grad_b, mixed, d_branch, errors,
-    proj, resid, weight, attention, branch, d_mixed,
-    load_sem, w_send, w_recv, e_send, e_recv,
+def anchor_of(errors, reference):
+    flat = errors[...].reshape(NZ * NY * NX * NC, 128)
+    total = jnp.sum(jnp.sum(flat, axis=0, keepdims=True), axis=1, keepdims=True)
+    known = jnp.sum(jnp.sum(reference[...], axis=0, keepdims=True), axis=1, keepdims=True)
+    return REWARD_SCALE * (known - total) / IMAGES
+
+
+def loss_of(error_row, slot, known, liked, anchor):
+    lane = lax.broadcasted_iota(jnp.int32, (1, 128), 1)
+    error = jnp.sum(jnp.where(lane == slot, error_row, 0.0), axis=1, keepdims=True)
+    sign = jnp.full((1, 1), 2 * liked - 1, jnp.int32).astype(F32)
+    reward = REWARD_SCALE * (jnp.full((1, 1), known, F32) - error)
+    sig = jax.nn.sigmoid(sign * (reward - anchor))
+    return 1.0 - sig, LOSS_SCALE * REWARD_SCALE * sign * sig * (1.0 - sig)
+
+
+def spread(stage, landed, sems, z, y, c, x):
+    rank = (z * NY + y) * NC + c
+
+    def step(n, carry):
+        k = (n * STRIDE) % DP
+        goal = (((z + k // (NY * NC)) % NZ) * NY + (y + (k // NC) % NY) % NY) * NC + (c + k % NC) % NC
+        remote(stage.at[goal], landed.at[rank], sems.at[0], sems.at[1], (goal, x)).start()
+        return carry
+
+    lax.fori_loop(1, DP, step, 0)
+    landed[rank] = stage[rank]
+    most = pl.ds(0, DP - 1)
+    return remote(stage.at[most], landed.at[most], sems.at[0], sems.at[1], ((rank + 1) % DP, x))
+
+
+def pick(landed, stage, senders):
+    def step(d, carry):
+        stage[d] = landed[senders[d]]
+        return carry
+
+    lax.fori_loop(0, DP, step, 0)
+
+
+def step_kernel(
+    proj_hbm, resid_hbm, weight_hbm, target, final, modulation, reference, sizes, steps, liked, known, senders,
+    grad_a, grad_b, grad_c, errors, out,
+    proj, resid, weight, attention, branch, d_mixed, mixed, d_branch,
+    stage_a, first_a, second_a, final_a, stage_b, first_b, second_b, final_b,
+    scaled, term, core_send, core_recv, own, far_send, far_recv, near_send, near_recv, y_total,
+    far_send_y, far_recv_y, near_send_y, near_recv_y, z_send, z_recv,
+    load_sem, w_send, w_recv, e_send, e_recv, move_sems, c_sems, x_sems, y_sems, z_sems,
 ):
     z, y, c, x = place()
-    dev = lax.axis_index("dp") * NX + x
+    rank = lax.axis_index("dp")
+    dev = rank * NX + x
     sibling = device(z, y, 1 - c, x)
     right, left = (x + 1) % NX, (x + NX - 1) % NX
     opposite = (x + 2) % NX
+    right_y, left_y = (y + 1) % NY, (y + NY - 1) % NY
     others_x = [device(z, y, c, (x + k) % NX) for k in range(1, NX)]
     others_y = [device(z, (y + k) % NY, c, x) for k in range(1, NY)]
     others_z = [device((z + k) % NZ, y, c, x) for k in range(1, NZ)]
+    x_pair = (device(z, y, c, right), device(z, y, c, left))
+    y_pair = (device(z, right_y, c, x), device(z, left_y, c, x))
 
     load_proj = pltpu.make_async_copy(proj_hbm, proj, load_sem.at[0])
     load_proj.start()
@@ -91,31 +144,60 @@
     load_weight = pltpu.make_async_copy(weight_hbm, weight.at[x], load_sem.at[2])
     load_weight.start()
 
-    greet([sibling] + others_x + others_y + others_z)
+    barrier = pltpu.get_barrier_semaphore()
+    for partner in others_x:
+        pl.semaphore_signal(barrier, inc=1, device_id=partner, device_id_type=MESH)
+
+    def hello(k, carry):
+        pl.semaphore_signal(barrier, inc=1, device_id=((rank + k) % DP, x), device_id_type=MESH)
+        return carry
+
+    lax.fori_loop(1, DP, hello, 0)
+    pl.semaphore_wait(barrier, DP - 1 + NX - 1)
 
     half = rows_of(c * HALF, HALF, 16)
     upper = rows_of(c * HALF, HALF // 2, 16)
     lower = rows_of(c * HALF + HALF // 2, HALF // 2, 16)
     mine = weight_hbm.at[half]
-    to_right = remote(mine, weight.at[x, half], w_send.at[0], w_recv.at[0], device(z, y, c, right))
-    to_left = remote(mine, weight.at[x, half], w_send.at[1], w_recv.at[1], device(z, y, c, left))
+    to_right = remote(mine, weight.at[x, half], w_send.at[0], w_recv.at[0], x_pair[0])
+    to_left = remote(mine, weight.at[x, half], w_send.at[1], w_recv.at[1], x_pair[1])
     to_right.start()
     to_left.start()
     load_proj.wait()
 
     first = longest(sizes, dev)
+    narrow = EARLY // 2 * HD
+    for side in range(2):
+        for base, low, count, rows in PARTS:
+            block = proj[first, SEQ - rows :, base + side * narrow : base + (side + 1) * narrow]
+            stage_a[side * 32 + low : side * 32 + low + count] = block.reshape(count, TILE, narrow)
+    move_1a = spread(stage_a, first_a, move_sems.at[0], z, y, c, x)
+
     root = 1.0 / math.sqrt(HD)
     key_index = lax.broadcasted_iota(jnp.int32, (LMAX, SEQ), 1)
+
+    def softmax(q, k, size):
+        scores = dot(q, k, 1, 1) * root
+        scores = jnp.where(key_index < TXT + size, scores, -1e30)
+        raised = jnp.exp(scores - jnp.max(scores, axis=-1, keepdims=True))
+        return raised * (1.0 / jnp.sum(raised, axis=-1, keepdims=True))
+
+    def gradients(q, k, v, probs, d_head):
+        d_probs = dot(d_head, v, 1, 1)
+        totals = jnp.sum(probs * d_probs, axis=-1, keepdims=True)
+        d_scores = (probs * (d_probs - totals) * root).astype(BF16)
+        return (
+            dot(d_scores, k, 1, 0).astype(BF16),
+            dot(d_scores, q, 0, 0).astype(BF16),
+            dot(probs.astype(BF16), d_head, 0, 0).astype(BF16),
+        )
 
     def head_forward(i, slot, size, h):
         cols = pl.multiple_of(h * HD, HD)
         q = proj[slot, pl.ds(TXT, LMAX), pl.ds(cols, HD)]
         k = proj[slot, :, pl.ds(D + cols, HD)]
         v = proj[slot, :, pl.ds(2 * D + cols, HD)]
-        scores = dot(q, k, 1, 1) * root
-        scores = jnp.where(key_index < TXT + size, scores, -1e30)
-        raised = jnp.exp(scores - jnp.max(scores, axis=-1, keepdims=True))
-        probs = raised * (1.0 / jnp.sum(raised, axis=-1, keepdims=True))
+        probs = softmax(q, k, size)
         attention[i, h] = probs
         mixed[rows_of(i * LMAX, LMAX, 16), pl.ds(cols, HD)] = dot(probs.astype(BF16), v, 1, 0).astype(BF16)
 
@@ -130,10 +212,10 @@
     lax.fori_loop(0, 2 * HEADS // GROUP, forward_group, 0)
 
     to_right.wait_recv()
-    on_right = remote(weight.at[left, upper], weight.at[left, upper], w_send.at[2], w_recv.at[2], device(z, y, c, right))
+    on_right = remote(weight.at[left, upper], weight.at[left, upper], w_send.at[2], w_recv.at[2], x_pair[0])
     on_right.start()
     to_left.wait_recv()
-    on_left = remote(weight.at[right, lower], weight.at[right, lower], w_send.at[3], w_recv.at[3], device(z, y, c, left))
+    on_left = remote(weight.at[right, lower], weight.at[right, lower], w_send.at[3], w_recv.at[3], x_pair[1])
     on_left.start()
     across = []
     for n, owner in enumerate((left, right)):
@@ -208,34 +290,29 @@
     for copy in e_x:
         copy.start()
 
-    def head_backward(i, slot, h, grads):
-        cols = pl.multiple_of(h * HD, HD)
+    def head_backward(i, slot, h, grads, moved=False):
+        cols = h * HD if moved else pl.multiple_of(h * HD, HD)
         q = proj[slot, pl.ds(TXT, LMAX), pl.ds(cols, HD)]
         k = proj[slot, :, pl.ds(D + cols, HD)]
         v = proj[slot, :, pl.ds(2 * D + cols, HD)]
         d_head = d_mixed[rows_of(i * LMAX, LMAX, 16), pl.ds(cols, HD)]
-        probs = attention[i, h]
-        d_probs = dot(d_head, v, 1, 1)
-        totals = jnp.sum(probs * d_probs, axis=-1, keepdims=True)
-        d_scores = (probs * (d_probs - totals) * root).astype(BF16)
         side = h // (HEADS // 2)
-        out_cols = rows_of((h % (HEADS // 2)) * HD, HD, 128)
-        d_q = dot(d_scores, k, 1, 0).astype(BF16)
-        d_k = dot(d_scores, q, 0, 0).astype(BF16)
-        d_v = dot(probs.astype(BF16), d_head, 0, 0).astype(BF16)
+        out_cols = pl.ds((h % (HEADS // 2)) * HD, HD) if moved else rows_of((h % (HEADS // 2)) * HD, HD, 128)
+        d_q, d_k, d_v = gradients(q, k, v, attention[i, h], d_head)
+        if moved:
+            pair, place_in = (h - EARLY) // 2, pl.ds((h - EARLY) % 2 * HD, HD)
+            for low, count, block in ((0, 8, d_q), (8, 12, d_k), (20, 12, d_v)):
+                for n in range(count):
+                    stage_b[2 * (low + n) + pair, :, place_in] = block[n * TILE : (n + 1) * TILE]
         grads[side, 0:8, :, out_cols] = d_q.reshape(8, 16, HD)
         grads[side, 8:20, :, out_cols] = d_k.reshape(12, 16, HD)
         grads[side, 20:32, :, out_cols] = d_v.reshape(12, 16, HD)
 
-    def backward(i, slot, grads):
-        def group(n, carry):
-            for j in range(GROUP):
-                head_backward(i, slot, n * GROUP + j, grads)
-            return carry
-
-        lax.fori_loop(0, HEADS // GROUP, group, 0)
-
-    backward(0, first, grad_a)
+    for h in range(EARLY, HEADS):
+        head_backward(0, first, h, grad_a, moved=True)
+    for h in range(EARLY):
+        for n in range(LMAX // TILE):
+            stage_b[n * EARLY + h, :, pl.ds(2 * HD, HD)] = d_mixed[pl.ds(n * TILE, TILE), pl.ds(h * HD, HD)]
 
     for copy in e_x:
         copy.wait_recv()
@@ -246,7 +323,8 @@
     for copy in e_y:
         copy.start()
 
-    backward(1, 1 - first, grad_b)
+    move_1a.wait_recv()
+    pick(first_a, second_a, senders)
 
     for copy in e_y:
         copy.wait_recv()
@@ -256,88 +334,53 @@
     ]
     for copy in e_z:
         copy.start()
+    move_2a = spread(second_a, final_a, move_sems.at[1], z, y, c, x)
+    move_1b = spread(stage_b, first_b, move_sems.at[2], z, y, c, x)
+
+    def backward(i, slot, grads, groups):
+        def group(n, carry):
+            for j in range(GROUP):
+                head_backward(i, slot, n * GROUP + j, grads)
+            return carry
+
+        lax.fori_loop(0, groups, group, 0)
+
+    backward(0, first, grad_a, EARLY // GROUP)
+    backward(1, 1 - first, grad_b, HEADS // GROUP)
+
     for copy in e_z:
         copy.wait_recv()
-    for copy in [to_right, to_left, on_right, on_left, last, e_core] + across + e_x + e_y + e_z:
-        copy.wait_send()
-
-
-def image_pass(projections, residual_in, velocity_target, out_weight, final_weight, modulation, sizes, steps):
-    grads = jax.ShapeDtypeStruct((2, 32, 16, HEADS // 2 * HD), BF16)
-    return pl.pallas_call(
-        image_kernel,
-        name="images",
-        out_shape=(
-            grads,
-            grads,
-            jax.ShapeDtypeStruct((2 * LMAX, D), BF16),
-            jax.ShapeDtypeStruct((2 * LMAX, D), BF16),
-            jax.ShapeDtypeStruct((NZ, NY, NX, NC, 1, 128), F32),
-        ),
-        in_specs=[ANY, ANY, ANY, VMEM, VMEM, VMEM, SMEM, SMEM],
-        out_specs=(VMEM,) * 5,
-        scratch_shapes=[
-            pltpu.VMEM((2, SEQ, 3 * D), BF16),
-            pltpu.VMEM((2, LMAX, D), BF16),
-            pltpu.VMEM((NX, D, COLS), BF16),
-            pltpu.VMEM((2, HEADS, LMAX, SEQ), F32),
-            pltpu.VMEM((2 * LMAX, D), F32),
-            pltpu.VMEM((2 * LMAX, D), BF16),
-            pltpu.SemaphoreType.DMA((3,)),
-            pltpu.SemaphoreType.DMA((7,)),
-            pltpu.SemaphoreType.DMA((7,)),
-            pltpu.SemaphoreType.DMA((14,)),
-            pltpu.SemaphoreType.DMA((14,)),
-        ],
-        compiler_params=pltpu.CompilerParams(
-            collective_id=0, has_side_effects=True, vmem_limit_bytes=VMEM_LIMIT
-        ),
-        cost_estimate=pl.CostEstimate(flops=4_500_000_000, bytes_accessed=20_000_000, transcendentals=600_000),
-    )(projections, residual_in, out_weight, velocity_target, final_weight, modulation, sizes, steps)
-
-
-def anchor_of(errors, reference):
-    flat = errors[...].reshape(NZ * NY * NX * NC, 128)
-    total = jnp.sum(jnp.sum(flat, axis=0, keepdims=True), axis=1, keepdims=True)
-    known = jnp.sum(jnp.sum(reference[...], axis=0, keepdims=True), axis=1, keepdims=True)
-    return REWARD_SCALE * (known - total) / IMAGES
-
-
-def loss_of(error_row, slot, known, liked, anchor):
-    lane = lax.broadcasted_iota(jnp.int32, (1, 128), 1)
-    error = jnp.sum(jnp.where(lane == slot, error_row, 0.0), axis=1, keepdims=True)
-    sign = jnp.full((1, 1), 2 * liked - 1, jnp.int32).astype(F32)
-    reward = REWARD_SCALE * (jnp.full((1, 1), known, F32) - error)
-    sig = jax.nn.sigmoid(sign * (reward - anchor))
-    return 1.0 - sig, LOSS_SCALE * REWARD_SCALE * sign * sig * (1.0 - sig)
-
-
-def weight_kernel(
-    mixed, d_branch, errors, reference, sizes, liked, known,
-    out,
-    scaled, term, core_send, core_recv, own, far_send, far_recv, near_send, near_recv, y_total,
-    far_send_y, far_recv_y, near_send_y, near_recv_y, z_send, z_recv,
-    c_sems, x_sems, y_sems, z_sems,
-):
-    z, y, c, x = place()
-    dev = lax.axis_index("dp") * NX + x
-    sibling = device(z, y, 1 - c, x)
-    right_x, left_x = (x + 1) % NX, (x + NX - 1) % NX
-    right_y, left_y = (y + 1) % NY, (y + NY - 1) % NY
-    x_pair = (device(z, y, c, right_x), device(z, y, c, left_x))
-    y_pair = (device(z, right_y, c, x), device(z, left_y, c, x))
-    others_z = [device((z + k) % NZ, y, c, x) for k in range(1, NZ)]
-    greet([sibling, *x_pair, *y_pair] + others_z)
 
     anchor = anchor_of(errors, reference)
     row = errors[z, y, x, c]
-    first = longest(sizes, dev)
     for i in range(2):
         slot = first if i == 0 else 1 - first
         index = 2 * dev + slot
         _, slope = loss_of(row, slot, known[index], liked[index], anchor)
         rows = pl.ds(i * LMAX, LMAX)
         scaled[rows, :] = (d_branch[rows, :].astype(F32) * slope).astype(BF16)
+
+    from_dev = senders[rank] * NX + x
+    third_size = sizes[2 * from_dev + longest(sizes, from_dev)]
+
+    def third_rows(h, part):
+        _, low, count, rows = PARTS[part]
+        base = h // (EARLY // 2) * 32 + low
+        return final_a[base : base + count, :, pl.ds(h % (EARLY // 2) * HD, HD)].reshape(rows, HD)
+
+    def third_forward():
+        move_2a.wait_recv()
+        for h in range(EARLY):
+            attention[0, h] = softmax(third_rows(h, 0), third_rows(h, 1), third_size)
+
+    def third_backward(h):
+        d_head = jnp.concatenate(
+            [final_b[n * EARLY + h, :, pl.ds(2 * HD, HD)] for n in range(LMAX // TILE)], axis=0
+        )
+        side, out_cols = h // (HEADS // 2), pl.ds((h % (HEADS // 2)) * HD, HD)
+        q, k, v = (third_rows(h, part) for part in range(3))
+        for (_, low, count, _), block in zip(PARTS, gradients(q, k, v, attention[0, h], d_head)):
+            grad_c[side, low : low + count, :, out_cols] = block.reshape(count, TILE, HD)
 
     def make(owner):
         term[...] = dot(mixed[...], scaled[:, rows_of(owner * COLS, COLS, 128)], 0, 0)
@@ -352,15 +395,14 @@
         copy.start()
         return copy
 
-    opposite = (x + 2) % NX
-    owners = (opposite, right_x, left_x, x)
+    owners = (opposite, right, left, x)
     copies = [make(owner) for owner in owners]
 
     def chip_total(n):
         copies[n].wait_recv()
         own[owners[n]] = own[owners[n]] + core_recv[owners[n]].astype(F32)
 
-    def ring(pair, sems, far, rights, lefts, far_out, far_in, near_out, near_in, size):
+    def ring(pair, sems, far, rights, lefts, far_out, far_in, near_out, near_in, size, between):
         middle = size // 2
         outer = []
         for n in range(2):
@@ -368,6 +410,7 @@
             copy = remote(far_out.at[n], far_in.at[n], sems.at[0, n], sems.at[1, n], pair[n])
             copy.start()
             outer.append(copy)
+        between()
         inner = []
         for n, near in ((0, rights), (1, lefts)):
             block = near()
@@ -394,8 +437,11 @@
 
     outer_x, inner_x = ring(
         x_pair, x_sems, lambda rows: own[opposite, rows, :], near_x(1), near_x(2),
-        far_send, far_recv, near_send, near_recv, HALF,
-    )
+        far_send, far_recv, near_send, near_recv, HALF, third_forward,
+    )
+    move_1b.wait_recv()
+    pick(first_b, second_b, senders)
+    move_2b = spread(second_b, final_b, move_sems.at[3], z, y, c, x)
     chip_total(3)
     inner_x[0].wait_recv()
     inner_x[1].wait_recv()
@@ -409,7 +455,7 @@
     outer_y, inner_y = ring(
         y_pair, y_sems, lambda rows: y_rows((y + 2) % NY, rows),
         lambda: lambda rows: y_rows(right_y, rows), lambda: lambda rows: y_rows(left_y, rows),
-        far_send_y, far_recv_y, near_send_y, near_recv_y, strip,
+        far_send_y, far_recv_y, near_send_y, near_recv_y, strip, lambda: None,
     )
     inner_y[0].wait_recv()
     inner_y[1].wait_recv()
@@ -430,19 +476,56 @@
         copy.wait_recv()
         total = total + z_recv[k]
     out[...] = total
+
+    move_2b.wait_recv()
+    for n in range(EARLY // GROUP):
+        for j in range(GROUP):
+            third_backward(n * GROUP + j)
+    for h in range(EARLY, HEADS):
+        pair, place_in = (h - EARLY) // 2, pl.ds((h - EARLY) % 2 * HD, HD)
+        out_cols = pl.ds((h % (HEADS // 2)) * HD, HD)
+        for n in range(32):
+            grad_c[h // (HEADS // 2), n, :, out_cols] = final_b[2 * n + pair, :, place_in]
+
     for copy in copies + outer_x + inner_x + outer_y + inner_y + z_copies:
         copy.wait_send()
-
-
-def weight_pass(mixed, d_branch, errors, reference, sizes, liked, known):
+    for copy in [to_right, to_left, on_right, on_left, last, e_core] + across + e_x + e_y + e_z:
+        copy.wait_send()
+    for copy in (move_1a, move_2a, move_1b, move_2b):
+        copy.wait_send()
+
+
+def step_pass(
+    projections, residual_in, velocity_target, out_weight, final_weight, modulation,
+    reference, sizes, steps, liked, known, senders,
+):
     strip = NZ * PART
+    grads = jax.ShapeDtypeStruct((2, 32, TILE, HEADS // 2 * HD), BF16)
+    chunks_a = pltpu.VMEM((DP, TILE, EARLY // 2 * HD), BF16)
+    chunks_b = pltpu.VMEM((DP, TILE, 3 * HD), BF16)
     return pl.pallas_call(
-        weight_kernel,
-        name="weight",
-        out_shape=jax.ShapeDtypeStruct((PART, COLS), F32),
-        in_specs=[VMEM, VMEM, VMEM, VMEM, SMEM, SMEM, SMEM],
-        out_specs=VMEM,
+        step_kernel,
+        name="step",
+        out_shape=(
+            grads,
+            grads,
+            grads,
+            jax.ShapeDtypeStruct((NZ, NY, NX, NC, 1, 128), F32),
+            jax.ShapeDtypeStruct((PART, COLS), F32),
+        ),
+        in_specs=[ANY, ANY, ANY, VMEM, VMEM, VMEM, VMEM] + [SMEM] * 5,
+        out_specs=(VMEM,) * 5,
         scratch_shapes=[
+            pltpu.VMEM((2, SEQ, 3 * D), BF16),
+            pltpu.VMEM((2, LMAX, D), BF16),
+            pltpu.VMEM((NX, D, COLS), BF16),
+            pltpu.VMEM((2, HEADS, LMAX, SEQ), F32),
+            pltpu.VMEM((2 * LMAX, D), F32),
+            pltpu.VMEM((2 * LMAX, D), BF16),
+            pltpu.VMEM((2 * LMAX, D), BF16),
+            pltpu.VMEM((2 * LMAX, D), BF16),
+            *[chunks_a] * 4,
+            *[chunks_b] * 4,
             pltpu.VMEM((2 * LMAX, D), BF16),
             pltpu.VMEM((D, COLS), F32),
             pltpu.VMEM((NX, HALF, COLS), BF16),
@@ -459,16 +542,25 @@
             pltpu.VMEM((2, strip, COLS), BF16),
             pltpu.VMEM((NZ, PART, COLS), F32),
             pltpu.VMEM((NZ - 1, PART, COLS), F32),
+            pltpu.SemaphoreType.DMA((3,)),
+            pltpu.SemaphoreType.DMA((7,)),
+            pltpu.SemaphoreType.DMA((7,)),
+            pltpu.SemaphoreType.DMA((14,)),
+            pltpu.SemaphoreType.DMA((14,)),
+            pltpu.SemaphoreType.DMA((4, 2)),
             pltpu.SemaphoreType.DMA((2, NX)),
             pltpu.SemaphoreType.DMA((2, 4)),
             pltpu.SemaphoreType.DMA((2, 4)),
             pltpu.SemaphoreType.DMA((2, NZ - 1)),
         ],
         compiler_params=pltpu.CompilerParams(
-            collective_id=1, has_side_effects=True, vmem_limit_bytes=VMEM_LIMIT
+            collective_id=0, has_side_effects=True, vmem_limit_bytes=VMEM_LIMIT
         ),
-        cost_estimate=pl.CostEstimate(flops=1_200_000_000, bytes_accessed=60_000_000, transcendentals=10),
-    )(mixed, d_branch, errors, reference, sizes, liked, known)
+        cost_estimate=pl.CostEstimate(flops=5_700_000_000, bytes_accessed=20_000_000, transcendentals=800_000),
+    )(
+        projections, residual_in, out_weight, velocity_target, final_weight, modulation,
+        reference, sizes, steps, liked, known, senders,
+    )
 
 
 def place_kernel(rank_ref, moves, sizes, liked, known, grad_a, grad_b, arrived, errors, reference, out, losses):
@@ -500,7 +592,7 @@
 
     def write(grads):
         for side in range(2):
-            for base, low, count, rows in ((0, 0, 8, LMAX), (D, 8, 12, SEQ), (2 * D, 20, 12, SEQ)):
+            for base, low, count, rows in PARTS:
                 block = grads[side, low : low + count].reshape(rows, wide).astype(F32) * slope
                 out[0, SEQ - rows :, base + side * wide : base + (side + 1) * wide] = block.astype(BF16)
         out[0, :TXT, :D] = jnp.zeros((TXT, D), BF16)
@@ -544,21 +636,15 @@
     reference = reference_error.reshape(4, 128)
     moves = move_list.reshape(-1)
     place_of = jnp.stack([rank, lax.axis_index("fsdp")]).astype(jnp.int32)
-    grad_a, grad_b, mixed, d_branch, errors = image_pass(
-        projections, residual_in, jnp.swapaxes(velocity_target, 1, 2), out_weight, final_weight.T,
-        modulation, bucket_sizes, timesteps,
-    )
-    spread = lax.all_to_all(
-        grad_a.reshape(senders, 16, -1), "dp", split_axis=0, concat_axis=0, tiled=True
-    )
     target_of = jnp.arange(senders, dtype=jnp.int32)[:, None] == move_list[0, :, 1][None, :]
     sender_rank = jnp.sum(jnp.where(target_of, move_list[0, :, 0][None, :], 0), axis=1)
-    picked = jnp.take(spread, sender_rank, axis=0, mode="clip")
-    arrived = lax.all_to_all(picked, "dp", split_axis=0, concat_axis=0, tiled=True)
-    weight_grad = weight_pass(mixed, d_branch, errors, reference, bucket_sizes, liked, reference_error)
+    grad_a, grad_b, grad_c, errors, weight_grad = step_pass(
+        projections, residual_in, jnp.swapaxes(velocity_target, 1, 2), out_weight, final_weight.T,
+        modulation, reference, bucket_sizes, timesteps, liked, reference_error, sender_rank,
+    )
     projection_grad, slot_loss = place_pass(
         place_of, moves, bucket_sizes, liked, reference_error,
-        grad_a, grad_b, arrived.reshape(grad_a.shape), errors, reference,
+        grad_a, grad_b, grad_c, errors, reference,
     )
     return (weight_grad, projection_grad, slot_loss)
 

time: 172 us -> 138 us (0.80); the launches traced: 172 us -> 136 us
  waiting for transfers between devices: 40 us -> 0 us
  Pallas kernels: 112 us -> 131 us
  starting transfers between devices: 13.8 us -> 0 us
    all_to_all x2 -> x0, waiting for transfers between devices: 40 us -> none  [the longest x1 40 us: local(): lax.all_to_all(grad_a.reshape(senders, 16, -1), 'dp', split_axis=0, conca...]
    pallas_call x2 -> x1, Pallas kernels: 106 us -> 125 us  [step_pass(): pl.pallas_call(step_kernel, name='step', out_shape=(grads, grads, grads,...]
    all_to_all x2 -> x0, starting transfers between devices: 13.8 us -> none  [the longest x1 8.33 us: local(): lax.all_to_all(grad_a.reshape(senders, 16, -1), 'dp', split_axis=0, conca...]
    gather x1 -> x0, local copies, waits for them, and re-layouts: 1.79 us -> none  [local(): picked = jnp.take(spread, sender_rank, axis=0, mode='clip')]
  transfers between devices with their start and end apart: 2 -> 0, of which waited for: 1 -> 0; matrix products, arithmetic and copies ran while one was open for 1% -> 0% of each run, Pallas kernels for 31% -> 0%
where the time goes in v2:
time: 138 us; the launch traced here: 136 us
  Pallas kernels  131 us (95%)
  local copies, waits for them, and re-layouts  2.75 us (2%)
    pallas_call x1, Pallas kernels, step_pass(): pl.pallas_call(step_kernel, name='step', out_shape=(grads, grads, grads,...  125 us
    pallas_call x1, Pallas kernels, place_pass(): pl.pallas_call(place_kernel, name='slots', grid=(3,), out_shape=(jax.Shap...  6.41 us

profile of v2, /device:TPU:4, one launch (start us, length us, event | category | flops | bytes accessed | tf_op | source)
XLA Modules:
  0.0 135.9 jit_solution(1360076153281779370)
XLA Ops:
  0.6 0.7 pad_add_fusion.rank_ref
  1.3 0.8 slice_bitcast_fusion.1
  2.1 0.6 select_reduce_fusion.senders
  2.7 0.8 copy.16
  3.4 0.6 reshape.15.moves
  4.0 124.8 %step.1 = (bf16[2,32,16,768]{3,2,1,0:T(8,128)(2,1)}, bf16[2,32,16,768]{3,2,1,0:T(8,128)(2,1)}, bf16[2,32,16,768]{3,2,1,0:T(8,128)(2,1)}, f32[8,4,4,2,1,128]{5,4,3,2,1,0:T(1,128)}, f32[24,384]{1,0:T(8,128)}) custom-call(bf16[2,192,4608]{2,1,0:T(8,128)(2,1)} %proj_hbm.1, bf16[2,192,1536]{2,1,0:T(8,128)(2,1)} %resid_hbm.1, bf16[1536,384]{1,0:T(8,128)(2,1)} %weight_hbm.1, ...), custom_call_target="tpu_custom_call" | custom-call | flops 5699999744 | bytes 20000000 | tf_op jit(solution)/shard_map/step/pallas_call | solution.py:506
  128.9 0.0 copy-start
  128.9 6.4 %slots.1 = (bf16[3,192,4608]{2,1,0:T(8,128)(2,1)}, f32[3]{0:T(128)}) custom-call(s32[2]{0:T(128)} %pad_add_fusion.rank_ref, s32[64]{0:T(128)} %reshape.15.moves, s32[512]{0:T(512)} %sizes.3, s32[512]{0:T(512)} %liked.3, f32[512]{0:T(512)} %known.3, bf16[2,32,16,768]{3,2,1,0:T(8,128)(2,1)} %get-tuple-element.11.grad_a, ...), custom_call_target="tpu_custom_call" | custom-call | flops 3000000 | bytes 10000000 | tf_op jit(solution)/shard_map/slots/pallas_call | solution.py:618
  135.3 0.0 copy-done
  135.3 0.6 copy.18
Async XLA Ops:
  128.9 6.4 %copy-start = (f32[24,384]{1,0:T(8,128)S(1)}, f32[24,384]{1,0:T(8,128)}, u32[]{:S(2)}) copy-start(f32[24,384]{1,0:T(8,128)} %get-tuple-element.22) | copy-start | bytes 110596

commit v3 on v2

v3 whole, which is shorter than its diff:
```python
import functools
import math

import jax
import jax.numpy as jnp
from jax import lax
from jax.experimental import pallas as pl
from jax.experimental.pallas import tpu as pltpu
from jax.sharding import PartitionSpec as P

HEADS = 12
HD = 128
D = 1536
PATCH = 64
TXT = 64
LMAX = 128
SEQ = 192
IMAGES = 512
NZ, NY, NC, NX = 8, 4, 2, 4
COLS = D // NX
HALF = D // NC
PART = 24
STRIP = NZ // 2 * PART
BLOCK = NY * STRIP
GROUP = 4
DP = NZ * NY * NC
EARLY = 8
TILE = 16

REWARD_SCALE = 2.0
LOSS_SCALE = 4096.0
EPSILON = 1e-06
MESH = pl.DeviceIdType.MESH
F32 = jnp.float32
BF16 = jnp.bfloat16
VMEM_LIMIT = 56 * 1024 * 1024

PARTS = ((0, 0, 8, LMAX), (D, 8, 12, SEQ), (2 * D, 20, 12, SEQ))

ANY = pl.BlockSpec(memory_space=pl.ANY)
VMEM = pl.BlockSpec(memory_space=pltpu.VMEM)
SMEM = pl.BlockSpec(memory_space=pltpu.SMEM)


def place():
    rank = lax.axis_index("dp")
    return lax.div(rank, NY * NC), lax.rem(lax.div(rank, NC), NY), lax.rem(rank, NC), lax.axis_index("fsdp")


def device(z, y, c, x):
    return ((z * NY + y) * NC + c, x)


def remote(src, dst, send, recv, target):
    return pltpu.make_async_remote_copy(
        src_ref=src, dst_ref=dst, send_sem=send, recv_sem=recv, device_id=target, device_id_type=MESH
    )


def dot(a, b, left, right):
    return lax.dot_general(a, b, (((left,), (right,)), ((), ())), preferred_element_type=F32)


def rows_of(start, size, step):
    return pl.ds(pl.multiple_of(start, step), size)


def longest(sizes, dev):
    return jnp.where(sizes[2 * dev] >= sizes[2 * dev + 1], 0, 1)


def anchor_of(errors, reference):
    flat = errors[...].reshape(DP * NX, 128)
    total = jnp.sum(jnp.sum(flat, axis=0, keepdims=True), axis=1, keepdims=True)
    known = jnp.sum(jnp.sum(reference[...], axis=0, keepdims=True), axis=1, keepdims=True)
    return REWARD_SCALE * (known - total) / IMAGES


def loss_of(error_row, slot, known, liked, anchor):
    lane = lax.broadcasted_iota(jnp.int32, (1, 128), 1)
    error = jnp.sum(jnp.where(lane == slot, error_row, 0.0), axis=1, keepdims=True)
    sign = jnp.full((1, 1), 2 * liked - 1, jnp.int32).astype(F32)
    reward = REWARD_SCALE * (jnp.full((1, 1), known, F32) - error)
    sig = jax.nn.sigmoid(sign * (reward - anchor))
    return 1.0 - sig, LOSS_SCALE * REWARD_SCALE * sign * sig * (1.0 - sig)


def partners(z, y, c):
    near = [lax.rem(y + k // NC, NY) * NC + lax.rem(c + k % NC, NC) for k in range(NY * NC)]

    def each(act):
        for place_in in near[1:]:
            act(z * (NY * NC) + place_in)

        def step(dz, carry):
            base = lax.rem(z + dz, NZ) * (NY * NC)
            for place_in in near:
                act(base + place_in)
            return carry

        lax.fori_loop(1, NZ, step, 0)

    return each


def spread(stage, landed, sems, rank, x, each):
    def send(goal):
        remote(stage.at[goal], landed.at[rank], sems.at[0], sems.at[1], (goal, x)).start()

    each(send)
    landed[rank] = stage[rank]
    most = pl.ds(0, DP - 1)
    return remote(stage.at[most], landed.at[most], sems.at[0], sems.at[1], (lax.rem(rank + 1, DP), x))


def pick(landed, stage, senders):
    def step(n, carry):
        for d in range(4):
            stage[4 * n + d] = landed[jnp.maximum(senders[4 * n + d], 0)]
        return carry

    lax.fori_loop(0, DP // 4, step, 0)


def step_kernel(
    proj_hbm, resid_hbm, weight_hbm, target, final, modulation, reference, sizes, steps, liked, known, senders,
    grads_hbm, errors, out, losses, factors, info,
    grads, proj, resid, weight, attention, branch, d_mixed, mixed, d_branch,
    stage_a, first_a0, first_a1, second_a, final_a, stage_d, first_d, second_d, final_d, stage_g, first_g, second_g, final_g,
    scaled, term, core_send, core_recv, own, far_send, far_recv, near_send, near_recv, y_total,
    far_send_2, far_recv_2, near_send_2, near_recv_2, z_send, z_recv,
    load_sem, save_sem, w_send, w_recv, e_sems, move_sems, c_sems, r_sems, z_sems,
):
    z, y, c, x = place()
    rank = lax.axis_index("dp")
    dev = rank * NX + x
    sibling = device(z, y, 1 - c, x)
    right, left = (x + 1) % NX, (x + NX - 1) % NX
    opposite = (x + 2) % NX
    right_y, left_y = (y + 1) % NY, (y + NY - 1) % NY
    others_x = [device(z, y, c, (x + k) % NX) for k in range(1, NX)]
    others_z = [device((z + k) % NZ, y, c, x) for k in range(1, NZ)]
    x_pair = (device(z, y, c, right), device(z, y, c, left))
    y_pair = (device(z, right_y, c, x), device(z, left_y, c, x))
    sent = []

    load_proj = pltpu.make_async_copy(proj_hbm, proj, load_sem.at[0])
    load_proj.start()
    load_resid = pltpu.make_async_copy(resid_hbm.at[:, pl.ds(TXT, LMAX)], resid, load_sem.at[1])
    load_resid.start()
    load_weight = pltpu.make_async_copy(weight_hbm, weight.at[x], load_sem.at[2])
    load_weight.start()

    barrier = pltpu.get_barrier_semaphore()
    for partner in others_x:
        pl.semaphore_signal(barrier, inc=1, device_id=partner, device_id_type=MESH)

    each = partners(z, y, c)
    each(lambda goal: pl.semaphore_signal(barrier, inc=1, device_id=(goal, x), device_id_type=MESH))

    load_proj.wait()
    first = longest(sizes, dev)
    narrow = 2 * HD
    for s in range(2):
        for pair in range(2):
            cols = (2 * s + pair) * narrow
            for base, low, count, rows in PARTS:
                block = proj[first, SEQ - rows :, base + cols : base + cols + narrow]
                stage_a[s, pair * 32 + low : pair * 32 + low + count] = block.reshape(count, TILE, narrow)
    pl.semaphore_wait(barrier, DP - 1 + NX - 1)

    half = rows_of(c * HALF, HALF, 16)
    upper = rows_of(c * HALF, HALF // 2, 16)
    lower = rows_of(c * HALF + HALF // 2, HALF // 2, 16)
    mine = weight_hbm.at[half]
    to_right = remote(mine, weight.at[x, half], w_send.at[0], w_recv.at[0], x_pair[0])
    to_left = remote(mine, weight.at[x, half], w_send.at[1], w_recv.at[1], x_pair[1])
    to_right.start()
    to_left.start()

    def move(stage, landed, number):
        copy = spread(stage, landed, move_sems.at[number], rank, x, each)
        sent.append(copy)
        return copy

    first_a = (first_a0, first_a1)
    move_1a = [move(stage_a.at[s], first_a[s], s) for s in range(2)]
    move_2a = []

    def second_hop_a(s):
        move_1a[s].wait_recv()
        pick(first_a[s], second_a.at[s], senders)
        move_2a.append(move(second_a.at[s], final_a.at[s], 2 + s))

    root = 1.0 / math.sqrt(HD)
    key_index = lax.broadcasted_iota(jnp.int32, (LMAX, SEQ), 1)

    def softmax(q, k, size):
        scores = dot(q, k, 1, 1) * root
        scores = jnp.where(key_index < TXT + size, scores, -1e30)
        raised = jnp.exp(scores - jnp.max(scores, axis=-1, keepdims=True))
        return raised * (1.0 / jnp.sum(raised, axis=-1, keepdims=True))

    def gradients(q, k, v, probs, d_head):
        d_probs = dot(d_head, v, 1, 1)
        totals = jnp.sum(probs * d_probs, axis=-1, keepdims=True)
        d_scores = (probs * (d_probs - totals) * root).astype(BF16)
        return (
            dot(d_scores, k, 1, 0).astype(BF16),
            dot(d_scores, q, 0, 0).astype(BF16),
            dot(probs.astype(BF16), d_head, 0, 0).astype(BF16),
        )

    def rows_and_cols(i, h):
        cols = h * HD if isinstance(h, int) else pl.multiple_of(h * HD, HD)
        return rows_of(i * LMAX, LMAX, 16), pl.ds(cols, HD), cols

    def head_inputs(slot, cols):
        q = proj[slot, pl.ds(TXT, LMAX), pl.ds(cols, HD)]
        k = proj[slot, :, pl.ds(D + cols, HD)]
        v = proj[slot, :, pl.ds(2 * D + cols, HD)]
        return q, k, v

    def forward_group(n, carry):
        i = n // (HEADS // GROUP)
        slot = jnp.where(i == 0, first, 1 - first)
        size = sizes[2 * dev + slot]
        for j in range(GROUP):
            h = (n % (HEADS // GROUP)) * GROUP + j
            rows, out_cols, cols = rows_and_cols(i, h)
            q, k, v = head_inputs(slot, cols)
            probs = softmax(q, k, size)
            attention[i, h] = probs
            mixed[rows, out_cols] = dot(probs.astype(BF16), v, 1, 0).astype(BF16)
        return carry

    lax.fori_loop(0, 2 * HEADS // GROUP, forward_group, 0)

    to_right.wait_recv()
    on_right = remote(weight.at[left, upper], weight.at[left, upper], w_send.at[2], w_recv.at[2], x_pair[0])
    on_right.start()
    to_left.wait_recv()
    on_left = remote(weight.at[right, lower], weight.at[right, lower], w_send.at[3], w_recv.at[3], x_pair[1])
    on_left.start()
    across = []
    for n, owner in enumerate((left, right)):
        copy = remote(weight.at[owner, half], weight.at[owner, half], w_send.at[4 + n], w_recv.at[4 + n], sibling)
        copy.start()
        across.append(copy)
    load_weight.wait()
    load_resid.wait()

    def branch_part(owner):
        cols = rows_of(owner * COLS, COLS, 128)
        branch[:, cols] = dot(mixed[...], weight[owner], 1, 0)

    branch_part(x)
    second_hop_a(0)
    across[0].wait_recv()
    branch_part(left)
    across[1].wait_recv()
    branch_part(right)
    on_right.wait_recv()
    on_left.wait_recv()
    last = remote(weight.at[opposite, half], weight.at[opposite, half], w_send.at[6], w_recv.at[6], sibling)
    last.start()
    last.wait_recv()
    branch_part(opposite)
    sent.extend([to_right, to_left, on_right, on_left, last] + across)

    lane = lax.broadcasted_iota(jnp.int32, (1, 128), 1)
    row_index = lax.broadcasted_iota(jnp.int32, (PATCH, LMAX), 1)
    level = lax.broadcasted_iota(jnp.int32, (16, 32), 1)

    def image_middle(i, found):
        slot = jnp.where(i == 0, first, 1 - first)
        size = sizes[2 * dev + slot]
        chosen = dot((level == steps[2 * dev + slot]).astype(F32).astype(BF16), modulation[...], 1, 0)[0:1]
        gate = chosen[:, :D]
        shift = chosen[:, D : 2 * D]
        scale = 1.0 + chosen[:, 2 * D :]
        rows = rows_of(i * LMAX, LMAX, 16)
        residual = resid[slot].astype(F32) + gate * branch[rows]
        centered = residual - jnp.mean(residual, axis=-1, keepdims=True)
        inverse = lax.rsqrt(jnp.mean(centered * centered, axis=-1, keepdims=True) + EPSILON)
        unit = centered * inverse
        normed = (unit * scale + shift).astype(BF16)
        predicted = dot(final[...], normed, 1, 1)
        differ = jnp.where(row_index < size, predicted - target[slot].astype(F32), 0.0)
        divisor = jnp.full((1, 1), PATCH * size, jnp.int32).astype(F32)
        squares = jnp.sum(jnp.sum(differ * differ, axis=1, keepdims=True), axis=0, keepdims=True)
        d_predicted = (differ * (2.0 / divisor)).astype(BF16)
        d_normed = dot(d_predicted, final[...], 0, 0) * scale
        d_residual = inverse * (
            d_normed
            - jnp.mean(d_normed, axis=-1, keepdims=True)
            - unit * jnp.mean(d_normed * unit, axis=-1, keepdims=True)
        )
        d_branch[rows, :] = (gate * d_residual).astype(BF16)
        return found + jnp.where(lane == slot, squares / divisor, 0.0)

    errors[rank, x] = lax.fori_loop(0, 2, image_middle, jnp.zeros((1, 128), F32))

    def hear(copies):
        for copy in copies:
            copy.wait_recv()

    e_x = [
        remote(errors.at[rank, x], errors.at[rank, x], e_sems.at[0, k], e_sems.at[1, k], goal)
        for k, goal in enumerate(others_x)
    ]
    for copy in e_x:
        copy.start()
    sent.extend(e_x)
    second_hop_a(1)

    total = dot(d_branch[:, pl.ds(0, COLS)], weight[0], 1, 1)
    for owner in range(1, NX):
        total += dot(d_branch[:, pl.ds(owner * COLS, COLS)], weight[owner], 1, 1)
    d_mixed[...] = total.astype(BF16)

    hear(e_x)
    each(
        lambda goal: remote(
            errors.at[rank], errors.at[rank], e_sems.at[0, NX - 1], e_sems.at[1, NX - 1], (goal, x)
        ).start()
    )
    most = pl.ds(0, DP - 1)
    e_all = remote(errors.at[most], errors.at[most], e_sems.at[0, NX - 1], e_sems.at[1, NX - 1], sibling)
    sent.append(e_all)

    for h in range(EARLY):
        for n in range(LMAX // TILE):
            stage_d[n * EARLY + h] = d_mixed[pl.ds(n * TILE, TILE), pl.ds(h * HD, HD)]
    move_1d = move(stage_d, first_d, 4)

    def store(i, h, blocks):
        side, out_cols = h // (HEADS // 2), rows_of((h % (HEADS // 2)) * HD, HD, HD)
        for (_, low, count, _), block in zip(PARTS, blocks):
            grads[i, side, low : low + count, :, out_cols] = block.reshape(count, TILE, HD)

    def head_backward(i, slot, h):
        rows, in_cols, cols = rows_and_cols(i, h)
        blocks = gradients(*head_inputs(slot, cols), attention[i, h], d_mixed[rows, in_cols])
        store(i, h, blocks)
        return blocks

    for h in range(EARLY, HEADS):
        blocks = head_backward(0, first, h)
        pair, place_in = (h - EARLY) // 2, pl.ds((h - EARLY) % 2 * HD, HD)
        for (_, low, count, _), block in zip(PARTS, blocks):
            stage_g[pair * 32 + low : pair * 32 + low + count, :, place_in] = block.reshape(count, TILE, HD)
    move_1g = move(stage_g, first_g, 5)
    e_all.wait_recv()

    anchor = anchor_of(errors, reference)
    origin = senders[rank]
    from_rank = jnp.maximum(origin, 0)
    from_dev = from_rank * NX + x
    from_slot = longest(sizes, from_dev)
    third_size = sizes[2 * from_dev + from_slot]

    def judge(row, slot, index):
        return loss_of(row, slot, known[index], liked[index], anchor)

    row = errors[rank, x]
    judged = [judge(row, slot, 2 * dev + slot) for slot in range(2)]
    judged.append(
        judge(
            errors[from_rank, x], from_slot, 2 * from_dev + from_slot
        )
    )
    for slot in range(3):
        loss, slope = judged[slot]
        here = origin >= 0 if slot == 2 else jnp.logical_or(origin >= 0, first != slot)
        losses[slot] = jnp.where(here, loss[0, 0], 0.0)
        factors[slot] = slope[0, 0]
        info[slot] = 2 if slot == 2 else jnp.where(first == slot, 0, 1)
        info[3 + slot] = jnp.where(here, 1, 0)

    for i in range(2):
        slope = jnp.where(first == i, judged[0][1], judged[1][1])
        rows = pl.ds(i * LMAX, LMAX)
        scaled[rows, :] = (d_branch[rows, :].astype(F32) * slope).astype(BF16)

    def make(owner):
        term[...] = dot(mixed[...], scaled[:, rows_of(owner * COLS, COLS, 128)], 0, 0)
        for p in range(2):
            for yy in range(NY):
                for core, goal in ((1 - c, core_send), (c, own)):
                    parts = [
                        term[rows_of(((zz * NY + yy) * NC + core) * PART, PART, 8), :]
                        for zz in range(p * NZ // 2, (p + 1) * NZ // 2)
                    ]
                    block = jnp.concatenate(parts, axis=0)
                    goal[owner, pl.ds((p * NY + yy) * STRIP, STRIP), :] = block.astype(goal.dtype)
        copy = remote(core_send.at[owner], core_recv.at[owner], c_sems.at[0, owner], c_sems.at[1, owner], sibling)
        copy.start()
        return copy

    owners = (opposite, right, left, x)
    copies = [make(owner) for owner in owners]
    sent.extend(copies)

    def chip_total(n):
        copies[n].wait_recv()
        own[owners[n]] = own[owners[n]] + core_recv[owners[n]].astype(F32)

    def ring_far(number, pair, block, bufs):
        far_out, far_in, _, _ = bufs
        outer = []
        for n in range(2):
            far_out[n] = block(n).astype(BF16)
            copy = remote(far_out.at[n], far_in.at[n], r_sems.at[number, 0, n], r_sems.at[number, 1, n], pair[n])
            copy.start()
            outer.append(copy)
        sent.extend(outer)
        return outer

    def ring_near(number, pair, outer, blocks, bufs):
        _, far_in, near_out, near_in = bufs
        middle = far_in.shape[1]
        inner = []
        for n in range(2):
            outer[n].wait_recv()
            for part in range(2):
                piece = blocks[n](part)
                if part == n:
                    piece = piece + far_in[n].astype(F32)
                near_out[n, pl.ds(part * middle, middle), :] = piece.astype(BF16)
            copy = remote(
                near_out.at[n], near_in.at[n], r_sems.at[number, 0, 2 + n], r_sems.at[number, 1, 2 + n], pair[n]
            )
            copy.start()
            inner.append(copy)
        sent.extend(inner)
        return inner

    def x_first(owner):
        return lambda part: own[owner, pl.ds(part * (BLOCK // 2), BLOCK // 2), :]

    def y_strip(which):
        return rows_of(BLOCK + which * STRIP, STRIP, 16)

    def y_first(which):
        return lambda part: jnp.concatenate([own[2 * part + n, y_strip(which), :] for n in range(2)], axis=0)

    def y_second(which):
        return lambda part: own[x, rows_of(which * STRIP + part * (STRIP // 2), STRIP // 2, 16), :]

    def x_second(owner):
        return lambda part: own[owner, rows_of(BLOCK + y * STRIP + part * (STRIP // 2), STRIP // 2, 16), :]

    bufs = [(far_send.at[n], far_recv.at[n], near_send.at[n], near_recv.at[n]) for n in range(2)]
    small = [(far_send_2.at[n], far_recv_2.at[n], near_send_2.at[n], near_recv_2.at[n]) for n in range(2)]
    chip_total(0)
    outer_x = ring_far(0, x_pair, x_first(opposite), bufs[0])
    chip_total(1)
    chip_total(2)
    chip_total(3)
    outer_y = ring_far(1, y_pair, y_first((y + 2) % NY), bufs[1])

    def backward(i, slot, groups):
        def group(n, carry):
            for j in range(GROUP):
                head_backward(i, slot, n * GROUP + j)
            return carry

        lax.fori_loop(0, groups, group, 0)

    backward(0, first, EARLY // GROUP)
    save = [pltpu.make_async_copy(grads.at[i], grads_hbm.at[i], save_sem.at[i]) for i in range(3)]
    save[0].start()
    inner_x = ring_near(0, x_pair, outer_x, (x_first(right), x_first(left)), bufs[0])
    inner_y = ring_near(1, y_pair, outer_y, (y_first(right_y), y_first(left_y)), bufs[1])
    backward(1, 1 - first, HEADS // GROUP)
    save[1].start()

    def third_rows(h, part):
        _, low, count, rows = PARTS[part]
        base = h % 4 // 2 * 32 + low
        return final_a[h // 4, base : base + count, :, pl.ds(h % 2 * HD, HD)].reshape(rows, HD)

    for s in range(2):
        move_2a[s].wait_recv()
        for h in range(4 * s, 4 * s + 4):
            attention[0, h] = softmax(third_rows(h, 0), third_rows(h, 1), third_size)

    move_1d.wait_recv()
    pick(first_d, second_d, senders)
    move_2d = move(second_d, final_d, 6)

    hear(inner_x)
    whole = pl.ds(0, BLOCK)
    own[x, whole, :] = own[x, whole, :] + near_recv[0, 0].astype(F32) + near_recv[0, 1].astype(F32)
    outer_y2 = ring_far(2, y_pair, y_second((y + 2) % NY), small[0])
    hear(inner_y)
    for owner in range(NX):
        rows = pl.ds(owner * STRIP, STRIP)
        own[owner, y_strip(y), :] = (
            own[owner, y_strip(y), :] + near_recv[1, 0, rows, :].astype(F32) + near_recv[1, 1, rows, :].astype(F32)
        )
    outer_x2 = ring_far(3, x_pair, x_second(opposite), small[1])

    move_1g.wait_recv()
    pick(first_g, second_g, senders)
    move_2g = move(second_g, final_g, 7)

    inner_y2 = ring_near(2, y_pair, outer_y2, (y_second(right_y), y_second(left_y)), small[0])
    inner_x2 = ring_near(3, x_pair, outer_x2, (x_second(right), x_second(left)), small[1])
    hear(inner_y2 + inner_x2)
    for p, rows in enumerate((rows_of(y * STRIP, STRIP, 16), y_strip(y))):
        y_total[pl.ds(p * STRIP, STRIP), :] = (
            own[x, rows, :] + near_recv_2[p, 0].astype(F32) + near_recv_2[p, 1].astype(F32)
        )
    for zz in range(NZ):
        block = jnp.concatenate([y_total[pl.ds(zz * PART, PART), :], jnp.zeros((8, COLS), F32)], axis=0)
        z_send[zz] = block.astype(BF16)
    z_copies = []
    for k in range(1, NZ):
        copy = remote(
            z_send.at[(z + k) % NZ], z_recv.at[k - 1], z_sems.at[0, k - 1], z_sems.at[1, k - 1], others_z[k - 1]
        )
        copy.start()
        z_copies.append(copy)
    sent.extend(z_copies)

    move_2d.wait_recv()
    for h in range(EARLY):
        d_head = jnp.concatenate([final_d[n * EARLY + h] for n in range(LMAX // TILE)], axis=0)
        store(2, h, gradients(*[third_rows(h, part) for part in range(3)], attention[0, h], d_head))

    total = y_total[rows_of(z * PART, PART, 8), :]
    for k, copy in enumerate(z_copies):
        copy.wait_recv()
        total = total + z_recv[k].astype(F32)[:PART]
    out[...] = total

    move_2g.wait_recv()
    for h in range(EARLY, HEADS):
        pair, place_in = (h - EARLY) // 2, pl.ds((h - EARLY) % 2 * HD, HD)
        out_cols = pl.ds((h % (HEADS // 2)) * HD, HD)
        grads[2, h // (HEADS // 2), :, :, out_cols] = final_g[pair * 32 : pair * 32 + 32, :, place_in]
    save[2].start()
    for copy in sent:
        copy.wait_send()
    for copy in save:
        copy.wait()


def step_pass(
    projections, residual_in, velocity_target, out_weight, final_weight, modulation,
    reference, sizes, steps, liked, known, senders,
):
    stack = (3, 2, 32, TILE, HEADS // 2 * HD)
    both = pltpu.VMEM((2, DP, TILE, 2 * HD), BF16)
    one = pltpu.VMEM((DP, TILE, 2 * HD), BF16)
    early = [both, one, one, both, both]
    middle = [pltpu.VMEM((DP, TILE, HD), BF16)] * 4
    late = [pltpu.VMEM((DP, TILE, 2 * HD), BF16)] * 4
    return pl.pallas_call(
        step_kernel,
        name="step",
        out_shape=(
            jax.ShapeDtypeStruct(stack, BF16),
            jax.ShapeDtypeStruct((DP, NX, 1, 128), F32),
            jax.ShapeDtypeStruct((PART, COLS), F32),
            jax.ShapeDtypeStruct((3,), F32),
            jax.ShapeDtypeStruct((3,), F32),
            jax.ShapeDtypeStruct((6,), jnp.int32),
        ),
        in_specs=[ANY, ANY, ANY, VMEM, VMEM, VMEM, VMEM] + [SMEM] * 5,
        out_specs=(ANY, VMEM, VMEM, SMEM, SMEM, SMEM),
        scratch_shapes=[
            pltpu.VMEM(stack, BF16),
            pltpu.VMEM((2, SEQ, 3 * D), BF16),
            pltpu.VMEM((2, LMAX, D), BF16),
            pltpu.VMEM((NX, D, COLS), BF16),
            pltpu.VMEM((2, HEADS, LMAX, SEQ), F32),
            pltpu.VMEM((2 * LMAX, D), F32),
            pltpu.VMEM((2 * LMAX, D), BF16),
            pltpu.VMEM((2 * LMAX, D), BF16),
            pltpu.VMEM((2 * LMAX, D), BF16),
            *early,
            *middle,
            *late,
            pltpu.VMEM((2 * LMAX, D), BF16),
            pltpu.VMEM((D, COLS), F32),
            pltpu.VMEM((NX, HALF, COLS), BF16),
            pltpu.VMEM((NX, HALF, COLS), BF16),
            pltpu.VMEM((NX, HALF, COLS), F32),
            *[pltpu.VMEM((2, 2, BLOCK // 2, COLS), BF16)] * 2,
            *[pltpu.VMEM((2, 2, BLOCK, COLS), BF16)] * 2,
            pltpu.VMEM((2 * STRIP, COLS), F32),
            *[pltpu.VMEM((2, 2, STRIP // 2, COLS), BF16)] * 2,
            *[pltpu.VMEM((2, 2, STRIP, COLS), BF16)] * 2,
            pltpu.VMEM((NZ, PART + 8, COLS), BF16),
            pltpu.VMEM((NZ - 1, PART + 8, COLS), BF16),
            pltpu.SemaphoreType.DMA((3,)),
            pltpu.SemaphoreType.DMA((3,)),
            pltpu.SemaphoreType.DMA((7,)),
            pltpu.SemaphoreType.DMA((7,)),
            pltpu.SemaphoreType.DMA((2, NX)),
            pltpu.SemaphoreType.DMA((8, 2)),
            pltpu.SemaphoreType.DMA((2, NX)),
            pltpu.SemaphoreType.DMA((4, 2, 4)),
            pltpu.SemaphoreType.DMA((2, NZ - 1)),
        ],
        compiler_params=pltpu.CompilerParams(
            collective_id=0, has_side_effects=True, vmem_limit_bytes=VMEM_LIMIT
        ),
        cost_estimate=pl.CostEstimate(flops=5_700_000_000, bytes_accessed=20_000_000, transcendentals=800_000),
    )(
        projections, residual_in, out_weight, velocity_target, final_weight, modulation,
        reference, sizes, steps, liked, known, senders,
    )


def place_kernel(info, factors, grads, out):
    slot = pl.program_id(0)
    wide = HEADS // 2 * HD

    @pl.when(info[3 + slot] == 0)
    def _():
        out[...] = jnp.zeros_like(out)

    @pl.when(info[3 + slot] == 1)
    def _():
        slope = jnp.full((1, 1), factors[slot], F32)
        for side in range(2):
            for base, low, count, rows in PARTS:
                block = grads[0, side, low : low + count].reshape(rows, wide).astype(F32) * slope
                out[0, SEQ - rows :, base + side * wide : base + (side + 1) * wide] = block.astype(BF16)
        out[0, :TXT, :D] = jnp.zeros((TXT, D), BF16)


def place_pass(info, factors, grads):
    return pl.pallas_call(
        place_kernel,
        name="slots",
        out_shape=jax.ShapeDtypeStruct((3, SEQ, 3 * D), BF16),
        grid_spec=pltpu.PrefetchScalarGridSpec(
            num_scalar_prefetch=2,
            grid=(3,),
            in_specs=[pl.BlockSpec((1, *grads.shape[1:]), lambda i, info, factors: (info[i], 0, 0, 0, 0))],
            out_specs=pl.BlockSpec((1, SEQ, 3 * D), lambda i, info, factors: (i, 0, 0)),
        ),
        compiler_params=pltpu.CompilerParams(vmem_limit_bytes=VMEM_LIMIT),
        cost_estimate=pl.CostEstimate(flops=3_000_000, bytes_accessed=10_000_000, transcendentals=10),
    )(info, factors, grads)


def local(
    projections, residual_in, velocity_target, out_weight, final_weight, modulation,
    bucket_sizes, liked, timesteps, reference_error, move_list,
):
    goal = jnp.arange(DP, dtype=jnp.int32)[:, None] == move_list[0, :, 1][None, :]
    senders = jnp.sum(jnp.where(goal, move_list[0, :, 0][None, :] + 1, 0), axis=1) - 1
    grads, _, weight_grad, slot_loss, factors, info = step_pass(
        projections, residual_in, jnp.swapaxes(velocity_target, 1, 2), out_weight, final_weight.T,
        modulation, reference_error.reshape(4, 128), bucket_sizes, timesteps, liked, reference_error, senders,
    )
    return (weight_grad, place_pass(info, factors, grads), slot_loss)


def solution(mesh):
    in_specs = (
        P(("dp", "fsdp"), None, None),
        P(("dp", "fsdp"), None, None),
        P(("dp", "fsdp"), None, None),
        P(None, "fsdp"),
        P(),
        P(),
        P(),
        P(),
        P(),
        P(),
        P("fsdp", None, None),
    )
    out_specs = (P("dp", "fsdp"), P(("dp", "fsdp"), None, None), P(("dp", "fsdp")))
    return jax.shard_map(local, mesh=mesh, in_specs=in_specs, out_specs=out_specs, check_vma=False)
```

time: 138 us -> 121 us (0.88); the launches traced: 136 us -> 121 us
  Pallas kernels: 131 us -> 118 us
  local copies, waits for them, and re-layouts: 2.75 us -> 1.14 us
    pallas_call x2, Pallas kernels: 131 us -> 118 us  [the longest x1 111 us: step_pass(): pl.pallas_call(step_kernel, name='step', out_shape=(jax.ShapeDtypeStruct(...]
where the time goes in v3:
time: 121 us
  Pallas kernels  118 us (98%)
  other arithmetic  1.37 us (1%)
    pallas_call x1, Pallas kernels, step_pass(): pl.pallas_call(step_kernel, name='step', out_shape=(jax.ShapeDtypeStruct(...  111 us
    pallas_call x1, Pallas kernels, place_pass(): pl.pallas_call(place_kernel, name='slots', out_shape=jax.ShapeDtypeStruct...  6.62 us

profile of v3, /device:TPU:4, one launch (start us, length us, event | category | flops | bytes accessed | tf_op | source)
XLA Modules:
  0.0 121.0 jit_solution(3842430292042021983)
XLA Ops:
  0.6 0.8 slice_bitcast_fusion
  1.4 0.1 select_reduce_fusion
  1.5 0.5 broadcast_add_fusion.senders
  2.0 111.2 %step.1 = (bf16[3,2,32,16,768]{4,3,2,1,0:T(8,128)(2,1)}, f32[64,4,1,128]{3,2,1,0:T(1,128)}, f32[24,384]{1,0:T(8,128)}, f32[3]{0:T(128)}, f32[3]{0:T(128)}, /*index=5*/s32[6]{0:T(128)}) custom-call(bf16[2,192,4608]{2,1,0:T(8,128)(2,1)} %proj_hbm.1, bf16[2,192,1536]{2,1,0:T(8,128)(2,1)} %resid_hbm.1, bf16[1536,384]{1,0:T(8,128)(2,1)} %weight_hbm.1, ...), custom_call_target="tpu_custom_call" | custom-call | flops 5699999744 | bytes 20000000 | tf_op jit(solution)/shard_map/step/pallas_call | solution.py:561
  113.2 0.0 copy-start
  113.2 0.0 copy-start.1
  113.2 6.6 %slots.1 = bf16[3,192,4608]{2,1,0:T(8,128)(2,1)} custom-call(s32[6]{0:T(128)} %get-tuple-element.9.info, f32[3]{0:T(128)} %get-tuple-element.10.factors, bf16[3,2,32,16,768]{4,3,2,1,0:T(8,128)(2,1)} %get-tuple-element.11.grads), custom_call_target="tpu_custom_call" | custom-call | flops 3000000 | bytes 10000000 | tf_op jit(solution)/shard_map/slots/pallas_call | solution.py:638
  119.9 0.0 copy-done
  119.9 0.6 copy.16
  120.5 0.0 copy-done.1
  120.5 0.5 copy.17
Async XLA Ops:
  113.2 6.6 %copy-start = (f32[24,384]{1,0:T(8,128)S(1)}, f32[24,384]{1,0:T(8,128)}, u32[]{:S(2)}) copy-start(f32[24,384]{1,0:T(8,128)} %get-tuple-element.18) | copy-start | bytes 110596
  113.2 7.3 %copy-start.1 = (f32[3]{0:T(128)S(1)}, f32[3]{0:T(128)}, u32[]{:S(2)}) copy-start(f32[3]{0:T(128)} %get-tuple-element.20) | copy-start | bytes 40
